TPU v7x, 256 devices: a whole 4x4x8 slice. The times are simulated.
256 devices in a mesh: depth: 4 (over y), row: 4 (over x_hi, core), col: 16 (over x_lo, z).
Axes of the slice: x: 4 (x_hi: 2, x_lo: 2; x = x_hi * 2 + x_lo), y: 4, z: 8, core: 2. Of those that a mesh axis runs over, the one named last changes fastest.
Arguments:
- kept_half: bfloat16 [1536, 7168], P(('depth', 'col'), 'row'), may hold values from -6 to 6
- mixed_half: bfloat16 [1536, 7168], P(('depth', 'col'), 'row'), may hold values from -6 to 6
- grad_kept: bfloat16 [1536, 7168], P(('depth', 'col'), 'row'), may hold values from -6 to 6
- grad_mixed: bfloat16 [1536, 7168], P(('depth', 'col'), 'row'), may hold values from -6 to 6
- gate_weight: bfloat16 [7168, 14336], P('row', 'col'), may hold values from -0.0625 to 0.0625
- up_weight: bfloat16 [7168, 14336], P('row', 'col'), may hold values from -0.0625 to 0.0625
- down_weight: bfloat16 [14336, 7168], P('col', 'row'), may hold values from -0.046875 to 0.046875
Outputs:
- restored: bfloat16 [1536, 7168], P(('depth', 'col'), 'row')
- grad_input: bfloat16 [1536, 7168], P(('depth', 'col'), 'row')
- grad_gate: bfloat16 [4, 1792, 14336], P('row', 'depth', 'col')
- grad_up: bfloat16 [4, 1792, 14336], P('row', 'depth', 'col')
- grad_down: bfloat16 [14336, 4, 1792], P('col', 'row', 'depth')
All inputs are finite; a program needn't handle non-finite values.
Results may differ from a plain program's by a relative error of at most 0.027.
Values may be sent and summed in bfloat16 or wider, within the bound.
A program may use at most 128 MiB of HBM per device.

v0:
```python
import jax
import jax.numpy as jnp
from jax import lax
from jax.sharding import PartitionSpec as P


def swiglu_back(gate, up, d_hidden):
    logistic = jax.nn.sigmoid(gate)
    active = gate * logistic
    hidden = (active * up).astype(jnp.bfloat16)
    d_gate = (d_hidden * up * logistic * (1.0 + gate * (1.0 - logistic))).astype(jnp.bfloat16)
    d_up = (d_hidden * active).astype(jnp.bfloat16)
    return (hidden, d_gate, d_up)


def right_product(left, right):
    return lax.dot_general(
        left, right, (((1,), (1,)), ((), ())), preferred_element_type=jnp.float32
    )


def left_product(left, right):
    return lax.dot_general(
        left, right, (((0,), (0,)), ((), ())), preferred_element_type=jnp.float32
    )


def body(kept_half, mixed_half, grad_kept, grad_mixed, gate_weight, up_weight, down_weight):
    width = gate_weight.shape[1]
    features = kept_half.shape[1]
    kept_all, upstream = (
        lax.all_gather(kept_half, "col", axis=0, tiled=True),
        lax.all_gather(grad_mixed, "col", axis=0, tiled=True),
    )
    gate_part = jnp.dot(kept_all, gate_weight, preferred_element_type=jnp.float32)
    up_part = jnp.dot(kept_all, up_weight, preferred_element_type=jnp.float32)
    back_part = right_product(upstream, down_weight)
    sums = lax.psum_scatter(
        jnp.concatenate([gate_part, up_part, back_part], axis=1).astype(jnp.bfloat16),
        "row",
        scatter_dimension=0,
        tiled=True,
    ).astype(jnp.float32)
    hidden, d_gate, d_up = swiglu_back(
        sums[:, :width], sums[:, width : 2 * width], sums[:, 2 * width :]
    )
    hidden_all, dgate_all, dup_all = (
        lax.all_gather(hidden, "row", axis=0, tiled=True),
        lax.all_gather(d_gate, "row", axis=0, tiled=True),
        lax.all_gather(d_up, "row", axis=0, tiled=True),
    )
    branch = jnp.dot(hidden_all, down_weight, preferred_element_type=jnp.float32)
    back = right_product(dgate_all, gate_weight) + right_product(dup_all, up_weight)
    totals = lax.psum_scatter(
        jnp.concatenate([branch, back], axis=1).astype(jnp.bfloat16),
        "col",
        scatter_dimension=0,
        tiled=True,
    ).astype(jnp.float32)
    restored = (mixed_half.astype(jnp.float32) - totals[:, :features]).astype(jnp.bfloat16)
    grad_input = (grad_kept.astype(jnp.float32) + totals[:, features:]).astype(jnp.bfloat16)
    restored, grad_input = (restored, grad_input)
    gate_sum, up_sum, down_sum = (
        lax.psum_scatter(
            left_product(kept_all, dgate_all).astype(jnp.bfloat16),
            "depth",
            scatter_dimension=0,
            tiled=True,
        ).astype(jnp.float32),
        lax.psum_scatter(
            left_product(kept_all, dup_all).astype(jnp.bfloat16),
            "depth",
            scatter_dimension=0,
            tiled=True,
        ).astype(jnp.float32),
        lax.psum_scatter(
            left_product(hidden_all, upstream).astype(jnp.bfloat16),
            "depth",
            scatter_dimension=1,
            tiled=True,
        ).astype(jnp.float32),
    )
    grad_gate = gate_sum.astype(jnp.bfloat16)[None]
    grad_up = up_sum.astype(jnp.bfloat16)[None]
    grad_down = down_sum.astype(jnp.bfloat16)[:, None, :]
    return (restored, grad_input, grad_gate, grad_up, grad_down)


def solution(mesh):
    in_specs = (
        P(("depth", "col"), "row"),
        P(("depth", "col"), "row"),
        P(("depth", "col"), "row"),
        P(("depth", "col"), "row"),
        P("row", "col"),
        P("row", "col"),
        P("col", "row"),
    )
    out_specs = (
        P(("depth", "col"), "row"),
        P(("depth", "col"), "row"),
        P("row", "depth", "col"),
        P("row", "depth", "col"),
        P("col", "row", "depth"),
    )
    return jax.shard_map(body, mesh=mesh, in_specs=in_specs, out_specs=out_specs, check_vma=False)
```

profile of v0, /device:TPU:1, one launch (start us, length us, event | category | flops | bytes accessed | tf_op | source)
XLA Modules:
  0.0 446.4 jit_solution(12466398825880849805)
XLA Ops:
  7.2 0.0 copy-start
  7.2 0.0 all-gather.3.cloned.1.call-start
  7.2 0.7 all-gather.3.cloned.1.call-update
  7.9 0.0 all-gather.5.cloned.1.call-start
  8.0 0.7 all-gather.5.cloned.1.call-update
  8.7 0.0 reduce-scatter.10.cloned.1.call-start
  8.7 65.2 %all-gather.3.cloned.1.call-done = bf16[384,1792]{1,0:T(8,128)(2,1)} async-done(((bf16[24,1792]{1,0:T(8,128)(2,1)}), bf16[384,1792]{1,0:T(8,128)(2,1)}) %all-gather.3.cloned.1.call-update) | async-done | bytes 1376272 | tf_op jit(solution)/shard_map/all_gather | solution.py:32
  73.9 0.0 copy-start.8
  73.9 0.0 copy-start.11
  73.9 4.9 %convolution_convert_fusion.5 = bf16[384,896]{1,0:T(8,128)(2,1)} fusion(bf16[384,1792]{1,0:T(8,128)(2,1)} %all-gather.3.cloned.1.call-done, bf16[1792,896]{1,0:T(8,128)(2,1)} %param.12), kind=kOutput, calls=%fused_computation.11 | convolution fusion | flops 1233469440 | bytes 5275648 | tf_op jit(solution)/shard_map/dot_general | solution.py:36
  78.8 0.0 copy-done.8
  78.8 0.0 copy-done.11
  78.8 2.4 convolution_convert_fusion.6
  81.2 62.0 %all-gather.5.cloned.1.call-done = bf16[384,1792]{1,0:T(8,128)(2,1)} async-done(((bf16[24,1792]{1,0:T(8,128)(2,1)}), bf16[384,1792]{1,0:T(8,128)(2,1)}) %all-gather.5.cloned.1.call-update) | async-done | bytes 1376272 | tf_op jit(solution)/shard_map/all_gather | solution.py:33
  143.2 0.0 copy-done
  143.2 0.0 copy-start.4
  143.2 0.0 copy-start.5
  143.2 3.1 convolution_convert_fusion.4
  146.3 0.0 copy-done.4
  146.3 0.0 copy-done.5
  146.3 1.5 pad_maximum_fusion.1
  147.8 0.0 reduce-scatter.10.cloned.1.call-update
  147.8 0.0 reduce-scatter.12.cloned.1.call-start
  147.9 50.7 %reduce-scatter.10.cloned.1.call-done = bf16[96,2688]{1,0:T(8,128)(2,1)} async-done(((bf16[384,2688]{1,0:T(8,128)(2,1)}), bf16[96,2688]{1,0:T(8,128)(2,1)}) %reduce-scatter.10.cloned.1.call-update) | async-done | bytes 516112 | tf_op jit(solution)/shard_map/reduce_scatter | solution.py:38
  198.6 1.1 convert_element_type.51
  199.7 0.2 multiply_convert_fusion.2
  199.9 9.7 %all_gather.17 = bf16[384,896]{1,0:T(8,128)(2,1)S(1)} all-gather(bf16[96,896]{1,0:T(8,128)(2,1)S(1)} %get-tuple-element.15), channel_id=1, replica_groups=mesh['depth'=4,'row'=4,'col'=16] {'row'}, dimensions={0}, use_global_device_ids=true | all-gather | bytes 860160 | tf_op jit(solution)/shard_map/all_gather | solution.py:48
  209.6 0.0 copy-start.1
  209.6 9.7 %all_gather.18 = bf16[384,896]{1,0:T(8,128)(2,1)S(1)} all-gather(bf16[96,896]{1,0:T(8,128)(2,1)S(1)} %get-tuple-element.16), channel_id=1, replica_groups=mesh['depth'=4,'row'=4,'col'=16] {'row'}, dimensions={0}, use_global_device_ids=true | all-gather | bytes 860160 | tf_op jit(solution)/shard_map/all_gather | solution.py:49
  219.2 0.0 copy-start.2
  219.2 9.7 %all_gather.19 = bf16[384,896]{1,0:T(8,128)(2,1)S(1)} all-gather(bf16[96,896]{1,0:T(8,128)(2,1)S(1)} %get-tuple-element.17), channel_id=1, replica_groups=mesh['depth'=4,'row'=4,'col'=16] {'row'}, dimensions={0}, use_global_device_ids=true | all-gather | bytes 860160 | tf_op jit(solution)/shard_map/all_gather | solution.py:50
  228.9 0.0 copy-done.1
  228.9 1.6 convolution_convert_fusion.3
  230.5 0.0 copy-done.2
  230.5 0.5 copy-done.9
  231.1 1.6 fusion.6
  232.7 0.0 copy-done.3
  232.7 0.3 copy-done.10
  233.0 1.7 fusion.2
  234.7 1.7 pad_maximum_fusion
  236.4 0.0 reduce-scatter.12.cloned.1.call-update
  236.4 0.0 reduce-scatter.18.cloned.1.call-start
  236.5 5.1 %fusion.1 = bf16[1792,896]{0,1:T(8,128)(2,1)} fusion(bf16[384,896]{1,0:T(8,128)(2,1)} %copy-done.3, bf16[384,1792]{1,0:T(8,128)(2,1)} %all-gather.3.cloned.1.call-done), kind=kOutput, calls=%fused_computation.4 | convolution fusion | flops 1234731008 | bytes 5275648 | tf_op jit(solution)/shard_map/dot_general | solution.py:23
  241.6 5.6 %copy.18 = bf16[1792,896]{1,0:T(8,128)(2,1)} copy(bf16[1792,896]{0,1:T(8,128)(2,1)} %fusion.1) | data formatting | bytes 6422528
  247.2 0.0 reduce-scatter.18.cloned.1.call-update
  247.2 0.0 reduce-scatter.16.cloned.1.call-start
  247.3 5.1 %fusion = bf16[1792,896]{0,1:T(8,128)(2,1)} fusion(bf16[384,896]{1,0:T(8,128)(2,1)} %copy-done.2, bf16[384,1792]{1,0:T(8,128)(2,1)} %all-gather.3.cloned.1.call-done), kind=kOutput, calls=%fused_computation.3 | convolution fusion | flops 1234731008 | bytes 5275648 | tf_op jit(solution)/shard_map/dot_general | solution.py:23
  252.4 5.6 %copy.16 = bf16[1792,896]{1,0:T(8,128)(2,1)} copy(bf16[1792,896]{0,1:T(8,128)(2,1)} %fusion) | data formatting | bytes 6422528
  258.0 0.0 reduce-scatter.16.cloned.1.call-update
  258.1 0.2 reduce-scatter.14.cloned.1.call-start
  258.3 5.3 %convolution_convert_fusion = bf16[896,1792]{0,1:T(8,128)(2,1)} fusion(bf16[384,896]{1,0:T(8,128)(2,1)} %copy-done.1, bf16[384,1792]{1,0:T(8,128)(2,1)} %all-gather.5.cloned.1.call-done), kind=kOutput, calls=%fused_computation | convolution fusion | flops 1234731008 | bytes 5275648 | tf_op jit(solution)/shard_map/dot_general | solution.py:23
  263.5 0.0 reduce-scatter.14.cloned.1.call-update
  263.6 38.2 %reduce-scatter.12.cloned.1.call-done = bf16[24,3584]{1,0:T(8,128)(2,1)} async-done(((bf16[384,3584]{1,0:T(8,128)(2,1)}), bf16[24,3584]{1,0:T(8,128)(2,1)}) %reduce-scatter.12.cloned.1.call-update) | async-done | bytes 172048 | tf_op jit(solution)/shard_map/reduce_scatter | solution.py:54
  301.7 0.9 convert_element_type.55
  302.7 0.0 copy-done.6
  302.7 0.0 copy-done.7
  302.7 0.7 fusion.4
  303.4 48.2 %reduce-scatter.18.cloned.1.call-done = bf16[448,896]{1,0:T(8,128)(2,1)} async-done(((bf16[1792,896]{1,0:T(8,128)(2,1)}), bf16[448,896]{1,0:T(8,128)(2,1)}) %reduce-scatter.18.cloned.1.call-update) | async-done | bytes 802832
  351.6 2.2 copy.19
  353.9 2.2 copy.15
  356.0 39.3 %reduce-scatter.16.cloned.1.call-done = bf16[448,896]{1,0:T(8,128)(2,1)} async-done(((bf16[1792,896]{1,0:T(8,128)(2,1)}), bf16[448,896]{1,0:T(8,128)(2,1)}) %reduce-scatter.16.cloned.1.call-update) | async-done | bytes 802832
  395.4 2.2 copy.17
  397.6 2.2 copy.14
  399.8 39.8 %reduce-scatter.14.cloned.1.call-done = bf16[896,448]{0,1:T(8,128)(2,1)} async-done(((bf16[896,1792]{0,1:T(8,128)(2,1)}), bf16[896,448]{0,1:T(8,128)(2,1)}) %reduce-scatter.14.cloned.1.call-update) | async-done | bytes 802832 | tf_op jit(solution)/shard_map/reduce_scatter | solution.py:76
  (5 shorter events, 0.0 us)
Async XLA Ops:
  7.2 136.1 %copy-start = (bf16[896,1792]{1,0:T(8,128)(2,1)S(1)}, bf16[896,1792]{1,0:T(8,128)(2,1)}, u32[]{:S(2)}) copy-start(bf16[896,1792]{1,0:T(8,128)(2,1)} %param.13) | copy-start | bytes 9633796
  7.2 66.7 %all-gather.3.cloned.1.call-start = ((), (), s32[]{:S(2)}) async-start(), calls=%async_computation.5 | async-start | bytes 1462272 | tf_op jit(solution)/shard_map/all_gather | solution.py:32
  7.9 135.3 %all-gather.5.cloned.1.call-start = ((), (), s32[]{:S(2)}) async-start(), calls=%async_computation.6 | async-start | bytes 1462272 | tf_op jit(solution)/shard_map/all_gather | solution.py:33
  8.7 189.9 %reduce-scatter.10.cloned.1.call-start = ((), (), s32[]{:S(2)}) async-start(), calls=%async_computation.7 | async-start | bytes 2580480 | tf_op jit(solution)/shard_map/reduce_scatter | solution.py:38
  73.9 4.9 %copy-start.8 = (bf16[1792,896]{1,0:T(8,128)(2,1)S(1)}, bf16[1792,896]{1,0:T(8,128)(2,1)}, u32[]{:S(2)}) copy-start(bf16[1792,896]{1,0:T(8,128)(2,1)} %param.11) | copy-start | bytes 9633796
  73.9 4.9 %copy-start.11 = (bf16[384,1792]{1,0:T(8,128)(2,1)S(1)}, bf16[384,1792]{1,0:T(8,128)(2,1)}, u32[]{:S(2)}) copy-start(bf16[384,1792]{1,0:T(8,128)(2,1)} %all-gather.3.cloned.1.call-done) | copy-start | bytes 4128772
  143.2 3.1 copy-start.4
  143.2 3.1 copy-start.5
  147.8 153.9 %reduce-scatter.12.cloned.1.call-start = ((), (), s32[]{:S(2)}) async-start(), calls=%async_computation.8 | async-start | bytes 2924544 | tf_op jit(solution)/shard_map/reduce_scatter | solution.py:54
  209.6 19.4 %copy-start.1 = (bf16[384,896]{1,0:T(8,128)(2,1)}, bf16[384,896]{1,0:T(8,128)(2,1)S(1)}, u32[]{:S(2)}) copy-start(bf16[384,896]{1,0:T(8,128)(2,1)S(1)} %all_gather.17) | copy-start | bytes 2064388
  219.2 11.3 %copy-start.2 = (bf16[384,896]{1,0:T(8,128)(2,1)}, bf16[384,896]{1,0:T(8,128)(2,1)S(1)}, u32[]{:S(2)}) copy-start(bf16[384,896]{1,0:T(8,128)(2,1)S(1)} %all_gather.18) | copy-start | bytes 2064388
  228.9 3.8 copy-start.3
  228.9 2.2 copy-start.9
  231.1 1.9 copy-start.10
  236.4 115.2 %reduce-scatter.18.cloned.1.call-start = ((), (), s32[]{:S(2)}) async-start(), calls=%async_computation.11 | async-start | bytes 4014080
  247.2 148.1 %reduce-scatter.16.cloned.1.call-start = ((), (), s32[]{:S(2)}) async-start(), calls=%async_computation.10 | async-start | bytes 4014080
  258.1 181.5 %reduce-scatter.14.cloned.1.call-start = ((), (), s32[]{:S(2)}) async-start(), calls=%async_computation.9 | async-start | bytes 4014080 | tf_op jit(solution)/shard_map/reduce_scatter | solution.py:76
  263.5 39.1 %copy-start.6 = (bf16[24,1792]{1,0:T(8,128)(2,1)S(1)}, bf16[24,1792]{1,0:T(8,128)(2,1)}, u32[]{:S(2)}) copy-start(bf16[24,1792]{1,0:T(8,128)(2,1)} %param.9) | copy-start | bytes 258052
  263.5 39.2 %copy-start.7 = (bf16[24,1792]{1,0:T(8,128)(2,1)S(1)}, bf16[24,1792]{1,0:T(8,128)(2,1)}, u32[]{:S(2)}) copy-start(bf16[24,1792]{1,0:T(8,128)(2,1)} %param.8) | copy-start | bytes 258052
Sparse Core Ops, SparseCore 0:
  9.8 64.0 all-gather.2
  75.7 67.5 all-gather.4
  147.9 50.5 reduce-scatter.9
  236.6 65.1 reduce-scatter.11
  304.2 47.4 reduce-scatter.17
  354.2 41.0 reduce-scatter.15
  398.5 41.0 reduce-scatter.13
where the time goes:
time: 447 us; the launch traced here: 446 us
  waiting for transfers between devices  345 us (77%)
  matrix products  30.8 us (7%)
  blocking collectives  29 us (6%)
  local copies, waits for them, and re-layouts  20.9 us (5%)
  between operations  14.2 us (3%)
  other arithmetic  6.16 us (1%)
    unnamed x9, waiting for transfers between devices  89 us
    all_gather x1, waiting for transfers between devices, body(): lax.all_gather(kept_half, 'col', axis=0, tiled=True)  65.2 us
    all_gather x1, waiting for transfers between devices, body(): lax.all_gather(grad_mixed, 'col', axis=0, tiled=True)  62 us
    reduce_scatter x1, waiting for transfers between devices, body(): lax.psum_scatter(jnp.concatenate([gate_part, up_part, back_part], axis=1)...  50.7 us
    reduce_scatter x1, waiting for transfers between devices, body(): lax.psum_scatter(left_product(hidden_all, upstream).astype(jnp.bfloat16),...  39.8 us
    reduce_scatter x1, waiting for transfers between devices, body(): lax.psum_scatter(jnp.concatenate([branch, back], axis=1).astype(jnp.bfloa...  38.2 us
    unnamed x30, local copies, waits for them, and re-layouts  20.9 us
    dot_general x3, matrix products, left_product(): lax.dot_general(left, right, (((0,), (0,)), ((), ())), preferred_element_...  15.5 us
  transfers between devices with their start and end apart: 7, of which 7 were waited for; matrix products, arithmetic and copies ran while one was open for 10% of the time, Pallas kernels for 0%

commit v1 on v0

v1 whole, which is shorter than its diff:
```python
import jax
import jax.numpy as jnp
from jax import lax
from jax.experimental import pallas as pl
from jax.experimental.pallas import tpu as pltpu
from jax.sharding import PartitionSpec as P

BF = jnp.bfloat16
F32 = jnp.float32
OFFSETS = (0, -1, 1, -2, 2, -3, 3, 4)
POS = {o: p for p, o in enumerate(OFFSETS)}
MESSAGES = 120


def dot(a, b):
    return jnp.dot(a, b, preferred_element_type=F32)


def dot_nt(a, b):
    return lax.dot_general(a, b, (((1,), (1,)), ((), ())), preferred_element_type=F32)


def tile(j, size):
    return pl.ds(pl.multiple_of(j * size, size), size)


class Message:
    def __init__(self, out, land):
        self.out, self.land = out, land

    def start(self):
        self.out.start()
        return self

    def arrived(self):
        self.land.wait_recv()

    def sent(self):
        self.out.wait_send()


def kernel(
    kept, mixed, gkept, gmixed, gate_hbm, up_hbm, down_hbm,
    o_restored, o_grad_input, o_gate, o_up, o_down,
    w, dn, xs, xr, k, u, kt, ut, kta, uta,
    pg, pb, rg, rb, sg, sb, tg, tb, h, g,
    zb, zk, rbp, rbm, rkp, rkm, ys, yr, acc, acc_d,
    ss, rs, ls,
):
    d, r, c = lax.axis_index("depth"), lax.axis_index("row"), lax.axis_index("col")
    xh, co, xl, z = r // 2, r % 2, c // 8, c % 8
    F = w.shape[1] // 2
    D = w.shape[0]
    HD = D // 2
    T = 48
    R = 96
    Q = D // 4

    def at(depth=d, xhi=xh, core=co, xlo=xl, zz=z):
        return (depth, xhi * 2 + core, xlo * 8 + zz)

    z_next, z_prev = at(zz=(z + 1) % 8), at(zz=(z + 7) % 8)
    y_next, y_prev, y_far = (at(depth=(d + i) % 4) for i in (1, 3, 2))
    other_core, other_hi, other_lo = at(core=1 - co), at(xhi=1 - xh), at(xlo=1 - xl)

    copies = [
        pltpu.make_async_copy(gate_hbm, w.at[:, pl.ds(0, F)], ls.at[0]),
        pltpu.make_async_copy(up_hbm, w.at[:, pl.ds(F, F)], ls.at[1]),
        pltpu.make_async_copy(down_hbm, dn, ls.at[2]),
    ]
    for copy in copies:
        copy.start()

    messages = []

    def message(src, dst, device, land=None):
        i = len(messages)
        sems = dict(send_sem=ss.at[i], recv_sem=rs.at[i], device_id=device, device_id_type=pl.DeviceIdType.MESH)
        out = pltpu.make_async_remote_copy(src_ref=src, dst_ref=dst, **sems)
        into = out if land is None else pltpu.make_async_remote_copy(src_ref=src, dst_ref=land, **sems)
        m = Message(out, into)
        messages.append(m)
        return m

    def send(src, dst, device, land=None):
        return message(src, dst, device, land).start()

    pad = jnp.zeros((8, D), F32)
    own_k = kept[...].astype(F32)
    own_u = gmixed[...].astype(F32)
    xs[0] = jnp.concatenate([own_k, pad], axis=0).astype(BF)
    xs[1] = jnp.concatenate([own_u, pad], axis=0).astype(BF)

    barrier = pltpu.get_barrier_semaphore()
    partners = (z_next, z_prev, y_next, y_prev, y_far, other_core, other_hi, other_lo)
    for partner in partners:
        pl.semaphore_signal(barrier, inc=1, device_id=partner, device_id_type=pl.DeviceIdType.MESH)
    pl.semaphore_wait(barrier, len(partners))

    pair_k = send(xs.at[0], xr.at[0], other_lo)
    pair_u = send(xs.at[1], xr.at[1], other_lo)

    def join(mine, theirs):
        first = jnp.where(xl == 0, mine, theirs)
        second = jnp.where(xl == 0, theirs, mine)
        return jnp.concatenate([first, second], axis=0).astype(BF)

    def part(ref, offset, f):
        return ref.at[pl.ds(T * POS[offset], T), pl.ds(HD * f, HD)]

    def hop_plus(ref, hop, f):
        to = -hop if hop < 4 else 4
        return send(part(ref, 1 - hop, f), part(ref, to, f), z_next)

    def hop_minus(ref, hop, f):
        return send(part(ref, hop - 1, f), part(ref, hop, f), z_prev)

    def first_hop(ref):
        return {
            (s, f): hop(ref, 1, f) for f in (0, 1) for s, hop in (("+", hop_plus), ("-", hop_minus))
        }

    def next_hop(ref, flying, hop):
        after = {}
        for (s, f), m in flying.items():
            m.arrived()
            if hop < 3 or (hop == 3 and (s, f) in (("+", 0), ("-", 1))):
                after[s, f] = (hop_plus if s == "+" else hop_minus)(ref, hop + 1, f)
        return after

    def spread(src, turned, gathered, group):
        @pl.loop(0, D // 256)
        def _(j):
            turned[group, tile(j, 256), :] = src[pl.ds(128 * group, 128), tile(j, 256)].T

        out = []
        for slot, depth in ((1, (d + 1) % 4), (3, (d + 3) % 4), (2, (d + 2) % 4)):
            rows = pl.ds(pl.multiple_of(depth * Q, Q), Q)
            out.append(send(turned.at[group, rows], gathered.at[slot, group], at(depth=depth)))
        return out

    pair_k.arrived()
    k[pl.ds(0, T), :] = join(own_k, xr[0].astype(F32)[:24])
    fly = first_hop(k)
    pair_u.arrived()
    u[pl.ds(0, T), :] = join(own_u, xr[1].astype(F32)[:24])
    fly = next_hop(k, fly, 1)
    spread_k = spread(k, kt, kta, 0)
    fly = next_hop(k, fly, 2)
    fly_u = first_hop(u)
    fly = next_hop(k, fly, 3)
    spread_k += spread(k, kt, kta, 1)
    fly = next_hop(k, fly, 4)
    spread_k += spread(k, kt, kta, 2)

    def gate_up(lo, hi):
        @pl.loop(lo, hi)
        def _(j):
            pg[:, tile(j, 256)] = dot(k[...], w[:, tile(j, 256)]).astype(BF)

    fly_u = next_hop(u, fly_u, 1)
    spread_u = spread(u, ut, uta, 0)
    copies[0].wait()
    copies[1].wait()
    gate_up(0, 3)
    fly_u = next_hop(u, fly_u, 2)
    gate_up(3, 7)

    def rows_of(row):
        return pl.ds(pl.multiple_of(row * R, R), R)

    def core_sums(partial, received):
        return [
            send(partial.at[rows_of(2 * i + 1 - co)], received.at[i], other_core) for i in (0, 1)
        ]

    def hi_sums(flying, partial, received, summed, far):
        for m in flying:
            m.arrived()
        there = 1 - xh
        summed[...] = (partial[rows_of(2 * there + co), :].astype(F32) + received[there].astype(F32)).astype(BF)
        return send(summed, far, other_hi)

    def total(partial, received, far, lo, hi):
        cols = pl.ds(lo, hi - lo)
        return partial[rows_of(r), cols].astype(F32) + received[xh, :, cols].astype(F32) + far[:, cols].astype(F32)

    core_g = core_sums(pg, rg)
    fly_u = next_hop(u, fly_u, 3)
    spread_u += spread(u, ut, uta, 1)
    hi_g = hi_sums(core_g, pg, rg, sg, tg)
    fly_u = next_hop(u, fly_u, 4)

    copies[2].wait()

    @pl.loop(0, 2)
    def _(j):
        pb[pl.ds(pl.multiple_of(j * 192, 192), 192), :] = dot_nt(
            u[pl.ds(pl.multiple_of(j * 192, 192), 192), :], dn[...]
        ).astype(BF)

    core_b = core_sums(pb, rb)
    spread_u += spread(u, ut, uta, 2)
    hi_b = hi_sums(core_b, pb, rb, sb, tb)

    hi_g.arrived()
    gate = total(pg, rg, tg, 0, F)
    up = total(pg, rg, tg, F, 2 * F)
    logistic = jax.nn.sigmoid(gate)
    active = gate * logistic
    h[0, rows_of(r), :] = (active * up).astype(BF)

    def share(ref, row):
        chunk = ref.at[0, rows_of(row)]
        theirs = (row // 2) * 2 + 1 - co
        cores = send(chunk, chunk, other_core, ref.at[0, rows_of(theirs)])
        plus = send(chunk, ref.at[1, rows_of(row)], y_next)
        minus = send(chunk, ref.at[3, rows_of(row)], y_prev)
        return cores, plus, minus

    def swap(ref):
        chunk = ref.at[0, rows_of(r)]
        return send(chunk, chunk, other_hi, ref.at[0, rows_of(2 * (1 - xh) + co)])

    def pass_on(ref, row, plus, minus):
        first = pl.ds(pl.multiple_of(row * R, R), T)
        second = pl.ds(pl.multiple_of(row * R + T, T), T)
        theirs = (row // 2) * 2 + 1 - co
        plus.arrived()
        far_plus = send(ref.at[1, first], ref.at[2, first], y_next)
        minus.arrived()
        far_minus = send(ref.at[3, second], ref.at[2, second], y_prev)
        cores = [
            send(ref.at[q, rows_of(row)], ref.at[q, rows_of(row)], other_core, ref.at[q, rows_of(theirs)])
            for q in (1, 3)
        ]
        return far_plus, far_minus, cores

    def last(ref, row, far_plus, far_minus):
        theirs = (row // 2) * 2 + 1 - co
        far_plus.arrived()
        far_minus.arrived()
        return send(ref.at[2, rows_of(row)], ref.at[2, rows_of(row)], other_core, ref.at[2, rows_of(theirs)])

    r_far = 2 * (1 - xh) + co
    swap_h = swap(h)
    share_h = share(h, r)

    hi_b.arrived()
    back = total(pb, rb, tb, 0, F)
    g[0, rows_of(r), pl.ds(0, F)] = (back * up * logistic * (1.0 + gate * (1.0 - logistic))).astype(BF)
    g[0, rows_of(r), pl.ds(F, F)] = (back * active).astype(BF)
    swap_g = swap(g)
    share_g = share(g, r)

    swap_h.arrived()
    share_h2 = share(h, r_far)
    share_h[0].arrived()
    share_h2[0].arrived()

    def branch(half):
        rows = pl.ds(half * 192, 192)

        @pl.loop(0, 7)
        def _(j):
            zb[rows, tile(j, 256)] = dot(h[0, rows, :], dn[:, tile(j, 256)]).astype(BF)

    def grad_back(half):
        rows = pl.ds(half * 192, 192)

        @pl.loop(0, 7)
        def _(j):
            zk[rows, tile(j, 256)] = dot_nt(g[0, rows, :], w[tile(j, 256), :]).astype(BF)

    def ring_first(ref, plus, minus):
        return (
            send(part(ref, 4, 0), plus.at[0, :, pl.ds(0, HD)], z_next),
            send(part(ref, 4, 1), minus.at[0, :, pl.ds(HD, HD)], z_prev),
        )

    def ring_next(ref, plus, minus, flying, hop):
        out = []
        for m, received, sign, to, f in ((flying[0], plus, 1, z_next, 0), (flying[1], minus, -1, z_prev, 1)):
            rows = pl.ds(T * POS[sign * (4 - hop)], T)
            cols = pl.ds(HD * f, HD) if hop == 1 else pl.ds(0, D)
            m.arrived()
            ref[rows, cols] = (ref[rows, cols].astype(F32) + received[hop - 1, :, cols].astype(F32)).astype(BF)
            out.append(send(ref.at[rows], received.at[hop], to))
        return out

    branch(1)
    ring_b = ring_first(zb, rbp, rbm)
    branch(0)
    swap_g.arrived()
    share_g2 = share(g, r_far)
    ring_b = ring_next(zb, rbp, rbm, ring_b, 1)
    share_g[0].arrived()
    share_g2[0].arrived()
    grad_back(1)
    ring_k = ring_first(zk, rkp, rkm)
    ring_b = ring_next(zb, rbp, rbm, ring_b, 2)
    grad_back(0)
    ring_k = ring_next(zk, rkp, rkm, ring_k, 1)

    def weight_grads(q, grads, turned_k, turned_u):
        if grads:
            lhs = turned_k()

            @pl.loop(0, 7)
            def _(j):
                term = dot(lhs, g[q, :, tile(j, 256)])
                if q == 0:
                    acc[:, tile(j, 256)] = term
                else:
                    acc[:, tile(j, 256)] += term
        else:
            lhs = turned_u()
            term = dot(lhs, h[q])
            if q == 0:
                acc_d[...] = term
            else:
                acc_d[...] += term

    own_rows = pl.ds(pl.multiple_of(d * Q, Q), Q)

    def turned(q, mine, gathered):
        def load():
            if q == 0:
                return jnp.concatenate([mine[i, own_rows, :] for i in range(3)], axis=1)
            return jnp.concatenate([gathered[q, i] for i in range(3)], axis=1)

        return load

    def grads_of(q, grads):
        weight_grads(q, grads, turned(q, kt, kta), turned(q, ut, uta))

    far_h = pass_on(h, r, *share_h[1:])
    ring_b = ring_next(zb, rbp, rbm, ring_b, 3)
    far_h2 = pass_on(h, r_far, *share_h2[1:])
    ring_k = ring_next(zk, rkp, rkm, ring_k, 2)
    grads_of(0, False)
    grads_of(0, True)

    def ring_last(ref, plus, minus, flying, i):
        for m in flying:
            m.arrived()
        whole = ref[pl.ds(0, T), :].astype(F32) + plus[3].astype(F32) + minus[3].astype(F32)
        mine = jnp.where(xl == 0, whole[:24], whole[24:])
        theirs = jnp.where(xl == 0, whole[24:], whole[:24])
        ys[i] = jnp.concatenate([theirs, pad], axis=0).astype(BF)
        return mine, send(ys.at[i], yr.at[i], other_lo)

    far_g = pass_on(g, r, *share_g[1:])
    ring_k = ring_next(zk, rkp, rkm, ring_k, 3)
    mine_b, end_b = ring_last(zb, rbp, rbm, ring_b, 0)
    end_b.arrived()
    o_restored[...] = (mixed[...].astype(F32) - (mine_b + yr[0].astype(F32)[:24])).astype(BF)
    far_g2 = pass_on(g, r_far, *share_g2[1:])

    last_h = [last(h, r, *far_h[:2]), last(h, r_far, *far_h2[:2])]
    mine_k, end_k = ring_last(zk, rkp, rkm, ring_k, 1)
    end_k.arrived()
    o_grad_input[...] = (gkept[...].astype(F32) + (mine_k + yr[1].astype(F32)[:24])).astype(BF)

    for m in spread_u + spread_k + far_h[2] + far_h2[2]:
        m.arrived()
    grads_of(1, False)
    grads_of(3, False)
    for m in last_h:
        m.arrived()
    grads_of(2, False)
    o_down[...] = acc_d[...].T.astype(BF)
    for m in far_g[2] + far_g2[2]:
        m.arrived()
    grads_of(1, True)
    grads_of(3, True)
    for m in [last(g, r, *far_g[:2]), last(g, r_far, *far_g2[:2])]:
        m.arrived()
    grads_of(2, True)
    o_gate[0] = acc[:, pl.ds(0, F)].astype(BF)
    o_up[0] = acc[:, pl.ds(F, F)].astype(BF)
    for m in messages:
        m.sent()


def body(kept_half, mixed_half, grad_kept, grad_mixed, gate_weight, up_weight, down_weight):
    D, F = gate_weight.shape
    Q = D // 4
    vmem = pl.BlockSpec(memory_space=pltpu.VMEM)
    hbm = pl.BlockSpec(memory_space=pl.ANY)

    def buf(*shape, dtype=BF):
        return pltpu.VMEM(shape, dtype)

    scratch = [
        buf(D, 2 * F), buf(F, D),
        buf(2, 32, D), buf(2, 32, D),
        buf(384, D), buf(384, D),
        buf(3, D, 128), buf(3, D, 128),
        buf(4, 3, Q, 128), buf(4, 3, Q, 128),
        buf(384, 2 * F), buf(384, F),
        buf(2, 96, 2 * F), buf(2, 96, F),
        buf(96, 2 * F), buf(96, F), buf(96, 2 * F), buf(96, F),
        buf(4, 384, F), buf(4, 384, 2 * F),
        buf(384, D), buf(384, D),
        buf(4, 48, D), buf(4, 48, D), buf(4, 48, D), buf(4, 48, D),
        buf(2, 32, D), buf(2, 32, D),
        buf(Q, 2 * F, dtype=F32), buf(Q, F, dtype=F32),
        pltpu.SemaphoreType.DMA((MESSAGES,)),
        pltpu.SemaphoreType.DMA((MESSAGES,)),
        pltpu.SemaphoreType.DMA((3,)),
    ]
    tokens = kept_half.shape[0]
    *outs, grad_down = pl.pallas_call(
        kernel,
        out_shape=(
            jax.ShapeDtypeStruct((tokens, D), BF),
            jax.ShapeDtypeStruct((tokens, D), BF),
            jax.ShapeDtypeStruct((1, Q, F), BF),
            jax.ShapeDtypeStruct((1, Q, F), BF),
            jax.ShapeDtypeStruct((F, Q), BF),
        ),
        in_specs=[vmem] * 4 + [hbm] * 3,
        out_specs=[vmem] * 5,
        scratch_shapes=scratch,
        compiler_params=pltpu.CompilerParams(
            collective_id=0, has_side_effects=True, vmem_limit_bytes=60 * 1024 * 1024
        ),
    )(kept_half, mixed_half, grad_kept, grad_mixed, gate_weight, up_weight, down_weight)
    return (*outs, grad_down[:, None, :])


def solution(mesh):
    in_specs = (
        P(("depth", "col"), "row"),
        P(("depth", "col"), "row"),
        P(("depth", "col"), "row"),
        P(("depth", "col"), "row"),
        P("row", "col"),
        P("row", "col"),
        P("col", "row"),
    )
    out_specs = (
        P(("depth", "col"), "row"),
        P(("depth", "col"), "row"),
        P("row", "depth", "col"),
        P("row", "depth", "col"),
        P("col", "row", "depth"),
    )
    return jax.shard_map(body, mesh=mesh, in_specs=in_specs, out_specs=out_specs, check_vma=False)
```

time: 447 us -> 126 us (0.28)
  waiting for transfers between devices: 345 us -> 0 us
  Pallas kernels: 0 us -> 117 us
  matrix products: 30.8 us -> 0 us
  blocking collectives: 29 us -> 0 us
  between operations: 14.2 us -> 0.65 us
  local copies, waits for them, and re-layouts: 20.9 us -> 8.29 us
  other arithmetic: 6.16 us -> 0 us
    reduce_scatter x3 -> x0, waiting for transfers between devices: 129 us -> none  [the longest x1 50.7 us: body(): lax.psum_scatter(jnp.concatenate([gate_part, up_part, back_part], axis=1)...]
    all_gather x2 -> x0, waiting for transfers between devices: 127 us -> none  [the longest x1 65.2 us: body(): lax.all_gather(kept_half, 'col', axis=0, tiled=True)]
    pallas_call x0 -> x1, Pallas kernels: none -> 117 us  [body(): pl.pallas_call(kernel, out_shape=(jax.ShapeDtypeStruct((tokens, D), BF),...]
    unnamed x9 -> x0, waiting for transfers between devices: 89 us -> none
    dot_general x9 -> x0, matrix products: 30.8 us -> none  [the longest x3 15.5 us: left_product(): lax.dot_general(left, right, (((0,), (0,)), ((), ())), preferred_element_...]
    all_gather x3 -> x0, blocking collectives: 29 us -> none  [the longest x1 9.69 us: body(): lax.all_gather(hidden, 'row', axis=0, tiled=True)]
    unnamed x30 -> x7, local copies, waits for them, and re-layouts: 20.9 us -> 8.29 us
  transfers between devices with their start and end apart: 7 -> 0, of which waited for: 7 -> 0; matrix products, arithmetic and copies ran while one was open for 10% -> 0% of each run, Pallas kernels for 0% -> 0%
where the time goes in v1:
time: 126 us
  Pallas kernels  117 us (93%)
  local copies, waits for them, and re-layouts  8.29 us (7%)
    pallas_call x1, Pallas kernels, body(): pl.pallas_call(kernel, out_shape=(jax.ShapeDtypeStruct((tokens, D), BF),...  117 us
    unnamed x7, local copies, waits for them, and re-layouts  8.29 us

profile of v1, /device:TPU:1, one launch (start us, length us, event | category | flops | bytes accessed | tf_op | source)
XLA Modules:
  0.0 126.2 jit_solution(14943833407538242230)
XLA Ops:
  0.6 117.3 %shard_map.110 = (bf16[24,1792]{1,0:T(8,128)(2,1)}, bf16[24,1792]{1,0:T(8,128)(2,1)}, bf16[1,448,896]{2,1,0:T(8,128)(2,1)}, bf16[1,448,896]{2,1,0:T(8,128)(2,1)}, bf16[896,448]{1,0:T(8,128)(2,1)}) custom-call(bf16[24,1792]{1,0:T(8,128)(2,1)} %kept.1, bf16[24,1792]{1,0:T(8,128)(2,1)} %mixed.1, bf16[24,1792]{1,0:T(8,128)(2,1)} %gkept.1, ...), custom_call_target="tpu_custom_call" | custom-call | tf_op jit(solution)/shard_map/pallas_call | solution.py:414
  117.9 0.0 copy-start
  117.9 2.3 %copy.12 = bf16[896,1,448]{0,2,1:T(8,128)(2,1)} copy(bf16[896,1,448]{2,0,1:T(8,128)(2,1)} %bitcast.1) | data formatting | bytes 1605632
  120.2 1.5 %copy.17 = bf16[24,1792]{1,0:T(8,128)(2,1)} copy(bf16[24,1792]{1,0:T(8,128)(2,1)} %get-tuple-element.25) | data formatting | bytes 172032
  121.7 1.5 %copy.18 = bf16[24,1792]{1,0:T(8,128)(2,1)} copy(bf16[24,1792]{1,0:T(8,128)(2,1)} %get-tuple-element.26) | data formatting | bytes 172032
  123.2 2.1 %copy.19 = bf16[1,448,896]{2,1,0:T(8,128)(2,1)} copy(bf16[1,448,896]{2,1,0:T(8,128)(2,1)} %get-tuple-element.27) | data formatting | bytes 1605632
  125.3 0.0 copy-done
  125.3 0.9 copy.20
Async XLA Ops:
  117.9 7.4 %copy-start = (bf16[1,448,896]{2,1,0:T(8,128)(2,1)S(1)}, bf16[1,448,896]{2,1,0:T(8,128)(2,1)}, u32[]{:S(2)}) copy-start(bf16[1,448,896]{2,1,0:T(8,128)(2,1)} %get-tuple-element.28) | copy-start | bytes 2408452

commit v2 on v0

v2 whole, which is shorter than its diff:
```python
import jax
import jax.numpy as jnp
from jax import lax
from jax.experimental import pallas as pl
from jax.experimental.pallas import tpu as pltpu
from jax.sharding import PartitionSpec as P

BF = jnp.bfloat16
F32 = jnp.float32
OFFSETS = (0, -1, 1, -2, 2, -3, 3, 4)
POS = {o: p for p, o in enumerate(OFFSETS)}
MESSAGES = 136


def dot(a, b):
    return jnp.dot(a, b, preferred_element_type=F32)


def tile(j, size):
    return pl.ds(pl.multiple_of(j * size, size), size)


class Message:
    def __init__(self, out, land):
        self.out, self.land, self.done, self.gone = out, land, False, False

    def start(self):
        self.out.start()
        return self

    def arrived(self):
        if self.done:
            return
        self.done = True
        self.land.wait_recv()

    def sent(self):
        if not self.gone:
            self.gone = True
            self.out.wait_send()


def kernel(
    kept_hbm, mixed_hbm, gkept_hbm, gmixed_hbm, gate_hbm, up_hbm, down_hbm,
    restored_hbm, grad_input_hbm, gate_up_hbm, grad_down_hbm,
    kept, mixed, gkept, gmixed, o_restored, o_grad_input, o_gate_up, o_down,
    w, dn, wt, dnt, xs, xr, k, u, kt, ut, kta, uta,
    pg, pb, rg, rb, sg, sb, tg, tb, h, g,
    zb, zk, rbp, rbm, rkp, rkm, ys, yr, acc, acc_d,
    ss, rs, ls,
):
    d, r, c = lax.axis_index("depth"), lax.axis_index("row"), lax.axis_index("col")
    xh, co, xl, z = r // 2, r % 2, c // 8, c % 8
    F = w.shape[1] // 2
    D = w.shape[0]
    HD = D // 2
    T = 48
    Q = D // 4

    def at(depth=d, xhi=xh, core=co, xlo=xl, zz=z):
        return (depth, xhi * 2 + core, xlo * 8 + zz)

    z_next, z_prev = at(zz=(z + 1) % 8), at(zz=(z + 7) % 8)
    y_next, y_prev, y_far = (at(depth=(d + i) % 4) for i in (1, 3, 2))
    other_core, other_hi, other_lo = at(core=1 - co), at(xhi=1 - xh), at(xlo=1 - xl)

    barrier = pltpu.get_barrier_semaphore()
    partners = (z_next, z_prev, y_next, y_prev, y_far, other_core, other_hi, other_lo)
    for partner in partners:
        pl.semaphore_signal(barrier, inc=1, device_id=partner, device_id_type=pl.DeviceIdType.MESH)

    inputs = [
        pltpu.make_async_copy(src, dst, ls.at[3 + i])
        for i, (src, dst) in enumerate(
            ((kept_hbm, kept), (gmixed_hbm, gmixed), (mixed_hbm, mixed), (gkept_hbm, gkept))
        )
    ]
    for copy in inputs:
        copy.start()

    copies = [
        pltpu.make_async_copy(gate_hbm, w.at[:, pl.ds(0, F)], ls.at[0]),
        pltpu.make_async_copy(up_hbm, w.at[:, pl.ds(F, F)], ls.at[1]),
        pltpu.make_async_copy(down_hbm, dn, ls.at[2]),
    ]
    for copy in reversed(copies):
        copy.start()

    messages = []

    def message(src, dst, device, land=None):
        i = len(messages)
        sems = dict(send_sem=ss.at[i], recv_sem=rs.at[i], device_id=device, device_id_type=pl.DeviceIdType.MESH)
        out = pltpu.make_async_remote_copy(src_ref=src, dst_ref=dst, **sems)
        into = out if land is None else pltpu.make_async_remote_copy(src_ref=src, dst_ref=land, **sems)
        m = Message(out, into)
        messages.append(m)
        return m

    def send(src, dst, device, land=None):
        return message(src, dst, device, land).start()

    pad = jnp.zeros((8, D), F32)
    for copy in inputs[:2]:
        copy.wait()
    own_k = kept[...].astype(F32)
    own_u = gmixed[...].astype(F32)
    xs[0] = jnp.concatenate([own_k, pad], axis=0).astype(BF)
    xs[1] = jnp.concatenate([own_u, pad], axis=0).astype(BF)

    pl.semaphore_wait(barrier, len(partners))

    pair_k = send(xs.at[0], xr.at[0], other_lo)
    pair_u = send(xs.at[1], xr.at[1], other_lo)

    def join(mine, theirs):
        first = jnp.where(xl == 0, mine, theirs)
        second = jnp.where(xl == 0, theirs, mine)
        return jnp.concatenate([first, second], axis=0).astype(BF)

    def part(ref, offset, f):
        return ref.at[pl.ds(T * POS[offset], T), pl.ds(HD * f, HD)]

    def hop_plus(ref, hop, f):
        to = -hop if hop < 4 else 4
        return send(part(ref, 1 - hop, f), part(ref, to, f), z_next)

    def hop_minus(ref, hop, f):
        return send(part(ref, hop - 1, f), part(ref, hop, f), z_prev)

    def first_hop(ref, fs=(0, 1)):
        return {(s, f): hop(ref, 1, f) for f in fs for s, hop in (("+", hop_plus), ("-", hop_minus))}

    def next_hop(ref, flying, hop, fs=(0, 1)):
        after = {}
        for (s, f), m in flying.items():
            if f not in fs:
                continue
            m.arrived()
            if hop < 3 or (hop == 3 and (s, f) in (("+", 0), ("-", 1))):
                after[s, f] = (hop_plus if s == "+" else hop_minus)(ref, hop + 1, f)
        return after

    def spread(src, turned, gathered, group):
        @pl.loop(0, D // 256)
        def _(j):
            turned[group, tile(j, 256), :] = src[pl.ds(128 * group, 128), tile(j, 256)].T

        out = []
        for slot, depth in ((1, (d + 1) % 4), (3, (d + 3) % 4), (2, (d + 2) % 4)):
            rows = pl.ds(pl.multiple_of(depth * Q, Q), Q)
            out.append(send(turned.at[group, rows], gathered.at[slot, group], at(depth=depth)))
        return out

    def turn_w(lo, hi):
        @pl.loop(lo, hi)
        def _(j):
            wt[:, tile(j, 256)] = w[tile(j, 256), :].T

    def gate_up(half):
        rows = pl.ds(4 * T * half, 4 * T)
        pg[half] = dot(k[rows, :], w[...]).astype(BF).reshape(2, 2, T, 2 * F)

    def d_hidden(half):
        rows = pl.ds(4 * T * half, 4 * T)
        pb[half] = dot(u[rows, :], dnt[...]).astype(BF).reshape(2, 2, T, F)

    def core_sums(partial, received, half):
        return send(partial.at[half, :, 1 - co], received.at[half], other_core)

    def hi_sums(flying, partial, received, summed, far, half):
        flying.arrived()
        there = 1 - xh
        summed[half] = (partial[half, there, co].astype(F32) + received[half, there].astype(F32)).astype(BF)
        return send(summed.at[half], far.at[half], other_hi)

    def total(partial, received, far, half, lo, hi):
        cols = pl.ds(lo, hi - lo)
        return (
            partial[half, xh, co, :, cols].astype(F32)
            + received[half, xh, :, cols].astype(F32)
            + far[half, :, cols].astype(F32)
        )

    class Share:
        def __init__(self, ref, half):
            self.ref, self.half = ref, half
            own = ref.at[0, half, xh, co]
            self.swap = send(own, own, other_hi, ref.at[0, half, 1 - xh, co])
            self.cores = [send(own, own, other_core, ref.at[0, half, xh, 1 - co])]
            self.own = (send(own, ref.at[1, half, xh, co], y_next), send(own, ref.at[3, half, xh, co], y_prev))

        def second(self):
            ref, half = self.ref, self.half
            self.swap.arrived()
            far = ref.at[0, half, 1 - xh, co]
            self.cores.append(send(far, far, other_core, ref.at[0, half, 1 - xh, 1 - co]))
            self.far = (
                send(far, ref.at[1, half, 1 - xh, co], y_next),
                send(far, ref.at[3, half, 1 - xh, co], y_prev),
            )

        def here(self):
            for m in self.cores:
                m.arrived()

        def pass_on(self):
            ref, half = self.ref, self.half
            self.own[0].arrived()
            plus = send(ref.at[1, half, xh, co], ref.at[2, half, xh, co], y_next)
            self.far[1].arrived()
            minus = send(ref.at[3, half, 1 - xh, co], ref.at[2, half, 1 - xh, co], y_prev)
            self.last = (plus, minus)

        def end(self):
            pass

        def of(self, q):
            return self.last if q == 2 else (self.own[q // 2], self.far[q // 2])

    class Relay(Share):
        def second(self):
            ref, half = self.ref, self.half
            self.swap.arrived()
            far = ref.at[0, half, 1 - xh, co]
            self.cores.append(send(far, far, other_core, ref.at[0, half, 1 - xh, 1 - co]))
            self.crossed = {}

        def cross(self, q):
            mine = self.ref.at[q, self.half, xh, co]
            self.crossed[q] = send(mine, mine, other_hi, self.ref.at[q, self.half, 1 - xh, co])

        def pass_on(self):
            ref, half, last = self.ref, self.half, []
            for i, q, to in ((0, 1, y_next), (1, 3, y_prev)):
                self.own[i].arrived()
                cols = pl.ds(F * i, F)
                last.append(send(ref.at[q, half, xh, co, :, cols], ref.at[2, half, xh, co, :, cols], to))
                self.cross(q)
            self.last = last

        def end(self):
            for m in self.last:
                m.arrived()
            self.cross(2)

        def of(self, q):
            return (self.crossed[q],)

    def to_core(shares, q):
        for s in shares:
            for m in s.of(q):
                m.arrived()
        ref = shares[0].ref
        mine = ref.at[q, :, :, co]
        return send(mine, mine, other_core, ref.at[q, :, :, 1 - co])

    def branch(half):
        zb[pl.ds(4 * T * half, 4 * T), :] = dot(h[0, half].reshape(4 * T, F), dn[...]).astype(BF)

    def grad_back(half):
        zk[pl.ds(4 * T * half, 4 * T), :] = dot(g[0, half].reshape(4 * T, 2 * F), wt[...]).astype(BF)

    class Ring:
        def __init__(self, ref, plus, minus, i):
            self.ref, self.i = ref, i
            self.sides = (("+", plus, 1, z_next, 0), ("-", minus, -1, z_prev, 1))
            self.fly = {}
            for s, received, _, to, f in self.sides:
                cols = pl.ds(HD * f, HD)
                self.fly[s, f] = send(part(ref, 4, f), received.at[0, :, cols], to)

        def step(self, hop):
            ref, fly = self.ref, {}
            for turn in (0, 1):
                for s, received, sign, to, f in self.sides:
                    f = f if turn == 0 else 1 - f
                    rows, cols = pl.ds(T * POS[sign * (4 - hop)], T), pl.ds(HD * f, HD)
                    if (s, f) in self.fly:
                        self.fly[s, f].arrived()
                        ref[rows, cols] = (
                            ref[rows, cols].astype(F32) + received[hop - 1, :, cols].astype(F32)
                        ).astype(BF)
                    fly[s, f] = send(ref.at[rows, cols], received.at[hop, :, cols], to)
            self.fly = fly

        def last(self):
            self.mine, self.end = [], []
            (_, plus, _, _, _), (_, minus, _, _, _) = self.sides
            for f in (0, 1):
                cols = pl.ds(HD * f, HD)
                self.fly["+", f].arrived()
                self.fly["-", f].arrived()
                whole = (
                    self.ref[pl.ds(0, T), cols].astype(F32)
                    + plus[3, :, cols].astype(F32)
                    + minus[3, :, cols].astype(F32)
                )
                self.mine.append(jnp.where(xl == 0, whole[:24], whole[24:]))
                theirs = jnp.where(xl == 0, whole[24:], whole[:24])
                ys[self.i, f] = jnp.concatenate([theirs, pad[:, :HD]], axis=0).astype(BF)
                self.end.append(send(ys.at[self.i, f], yr.at[self.i, f], other_lo))

        def result(self, out, base, sign):
            for f in (0, 1):
                cols = pl.ds(HD * f, HD)
                self.end[f].arrived()
                whole = self.mine[f] + yr[self.i, f].astype(F32)[:24]
                out[:, cols] = (base[:, cols].astype(F32) + sign * whole).astype(BF)

    own_rows = pl.ds(pl.multiple_of(d * Q, Q), Q)

    def turned(q, mine, gathered):
        if q == 0:
            return [mine[i, own_rows, :] for i in range(3)]
        return [gathered[q, i] for i in range(3)]

    def grads_gate_up(qs, first=False, end=False):
        lhs = jnp.concatenate([x for q in qs for x in turned(q, kt, kta)], axis=1)
        rhs = jnp.concatenate([g[q].reshape(8 * T, 2 * F) for q in qs], axis=0)
        term = dot(lhs, rhs)
        if not first:
            term = term + acc[...]
        if end:
            o_gate_up[...] = term.astype(BF)
        else:
            acc[...] = term

    def grads_down(qs, first=False, end=False):
        lhs = jnp.concatenate([x for q in qs for x in turned(q, ut, uta)], axis=1)
        rhs = jnp.concatenate([h[q].reshape(8 * T, F) for q in qs], axis=0)
        term = dot(lhs, rhs)
        if not first:
            term = term + acc_d[...]
        if end:
            o_down[...] = term.astype(BF)
        else:
            acc_d[...] = term

    results = []

    def store(src, dst):
        results.append(pltpu.make_async_copy(src, dst, ls.at[7 + len(results)]))
        results[-1].start()

    def activate(hi, half):
        hi.arrived()
        gate = total(pg, rg, tg, half, 0, F)
        up = total(pg, rg, tg, half, F, 2 * F)
        logistic = jax.nn.sigmoid(gate)
        active = gate * logistic
        h[0, half, xh, co] = (active * up).astype(BF)
        return up * logistic * (1.0 + gate * (1.0 - logistic)), active

    def deactivate(hi, half, slope, active):
        hi.arrived()
        back = total(pb, rb, tb, half, 0, F)
        g[0, half, xh, co, :, pl.ds(0, F)] = (back * slope).astype(BF)
        g[0, half, xh, co, :, pl.ds(F, F)] = (back * active).astype(BF)

    copies[2].wait()

    @pl.loop(0, 7)
    def _(j):
        dnt[tile(j, 256), :] = dn[:, tile(j, 256)].T

    copies[0].wait()
    copies[1].wait()
    turn_w(0, 2)
    pair_k.arrived()
    k[pl.ds(0, T), :] = join(own_k, xr[0].astype(F32)[:24])
    fly = first_hop(k)
    pair_u.arrived()
    u[pl.ds(0, T), :] = join(own_u, xr[1].astype(F32)[:24])
    turn_w(2, 4)
    fly = next_hop(k, fly, 1)
    fly_u = first_hop(u, (0,))
    spread_k = spread(k, kt, kta, 0)
    turn_w(4, 6)
    fly = next_hop(k, fly, 2)
    fly_u |= first_hop(u, (1,))
    gate_up(0)
    core_g0 = core_sums(pg, rg, 0)
    fly = next_hop(k, fly, 3)
    fly_u0 = next_hop(u, fly_u, 1, (0,))
    spread_k += spread(k, kt, kta, 1)
    hi_g0 = hi_sums(core_g0, pg, rg, sg, tg, 0)
    fly_u1 = next_hop(u, fly_u, 1, (1,))
    fly = next_hop(k, fly, 4)
    gate_up(1)
    core_g1 = core_sums(pg, rg, 1)
    fly_u0 = next_hop(u, fly_u0, 2)
    spread_k += spread(k, kt, kta, 2)
    hi_g1 = hi_sums(core_g1, pg, rg, sg, tg, 1)
    fly_u1 = next_hop(u, fly_u1, 2)
    slope0, active0 = activate(hi_g0, 0)
    h0 = Share(h, 0)
    spread_u = spread(u, ut, uta, 0)
    d_hidden(0)
    core_b0 = core_sums(pb, rb, 0)
    fly_u0 = next_hop(u, fly_u0, 3)
    fly_u1 = next_hop(u, fly_u1, 3)
    hi_b0 = hi_sums(core_b0, pb, rb, sb, tb, 0)
    slope1, active1 = activate(hi_g1, 1)
    h1 = Share(h, 1)
    h0.second()
    next_hop(u, fly_u0, 4)
    next_hop(u, fly_u1, 4)
    d_hidden(1)
    core_b1 = core_sums(pb, rb, 1)
    deactivate(hi_b0, 0, slope0, active0)
    hi_b1 = hi_sums(core_b1, pb, rb, sb, tb, 1)
    g0 = Relay(g, 0)
    h1.second()
    h1.here()
    branch(1)
    ring_b = Ring(zb, rbp, rbm, 0)
    h0.here()
    branch(0)
    deactivate(hi_b1, 1, slope1, active1)
    g1 = Share(g, 1)
    spread_u += spread(u, ut, uta, 1)
    turn_w(6, 7)
    ring_b.step(1)
    g0.second()
    ring_b.step(2)
    g1.second()
    g1.here()
    grad_back(1)
    ring_k = Ring(zk, rkp, rkm, 1)
    g0.here()
    grad_back(0)
    ring_b.step(3)
    h0.pass_on()
    h1.pass_on()
    spread_u += spread(u, ut, uta, 2)
    ring_k.step(1)
    g0.pass_on()
    grads_gate_up([0], first=True)
    ring_b.last()
    ring_k.step(2)
    hq = [to_core((h0, h1), 1), to_core((h0, h1), 3)]
    g1.pass_on()
    grads_down([0], first=True)
    hq.append(to_core((h0, h1), 2))
    ring_k.step(3)
    g0.end()
    for m in spread_k + spread_u + hq[:2]:
        m.arrived()
    grads_down([1, 3])
    gq = [to_core((g0, g1), 1), to_core((g0, g1), 3)]
    for copy in inputs[2:]:
        copy.wait()
    ring_b.result(o_restored, mixed, -1.0)
    store(o_restored, restored_hbm)
    hq[2].arrived()
    grads_down([2], end=True)
    store(o_down, grad_down_hbm)
    for m in gq:
        m.arrived()
    grads_gate_up([1, 3])
    for m in messages:
        if m.done:
            m.sent()
    ring_k.last()
    to_core((g0, g1), 2).arrived()
    grads_gate_up([2], end=True)
    store(o_gate_up, gate_up_hbm)
    ring_k.result(o_grad_input, gkept, 1.0)
    store(o_grad_input, grad_input_hbm)
    for m in messages:
        m.sent()
    for copy in results:
        copy.wait()
    assert len(messages) <= MESSAGES


def hand_over(
    restored, grad_input, gate_up, down, o_restored, o_grad_input, o_gate, o_up, o_down,
    v_restored, v_grad_input, v_gate_up, v_down, sems,
):
    F = o_gate.shape[2]
    loads = [
        pltpu.make_async_copy(src, dst, sems.at[i])
        for i, (src, dst) in enumerate(
            ((gate_up, v_gate_up), (down, v_down), (restored, v_restored), (grad_input, v_grad_input))
        )
    ]
    for copy in loads:
        copy.start()
    stores = []
    for i, (load, src, dst) in enumerate(
        (
            (0, v_gate_up.at[:, pl.ds(0, F)], o_gate.at[0]),
            (None, v_gate_up.at[:, pl.ds(F, F)], o_up.at[0]),
            (1, v_down, o_down),
            (2, v_restored, o_restored),
            (3, v_grad_input, o_grad_input),
        )
    ):
        if load is not None:
            loads[load].wait()
        stores.append(pltpu.make_async_copy(src, dst, sems.at[4 + i]))
        stores[-1].start()
    for copy in stores:
        copy.wait()


def body(kept_half, mixed_half, grad_kept, grad_mixed, gate_weight, up_weight, down_weight):
    D, F = gate_weight.shape
    Q = D // 4
    T = 48
    hbm = pl.BlockSpec(memory_space=pl.ANY)

    def buf(*shape, dtype=BF):
        return pltpu.VMEM(shape, dtype)

    scratch = [
        *[buf(24, D)] * 6, buf(Q, 2 * F), buf(Q, F),
        buf(D, 2 * F), buf(F, D), buf(2 * F, D), buf(D, F),
        buf(2, 32, D), buf(2, 32, D),
        buf(384, D), buf(384, D),
        buf(3, D, 128), buf(3, D, 128),
        buf(4, 3, Q, 128), buf(4, 3, Q, 128),
        buf(2, 2, 2, T, 2 * F), buf(2, 2, 2, T, F),
        buf(2, 2, T, 2 * F), buf(2, 2, T, F),
        buf(2, T, 2 * F), buf(2, T, F), buf(2, T, 2 * F), buf(2, T, F),
        buf(4, 2, 2, 2, T, F), buf(4, 2, 2, 2, T, 2 * F),
        buf(384, D), buf(384, D),
        buf(4, T, D), buf(4, T, D), buf(4, T, D), buf(4, T, D),
        buf(2, 2, 32, D // 2), buf(2, 2, 32, D // 2),
        buf(Q, 2 * F, dtype=F32), buf(Q, F, dtype=F32),
        pltpu.SemaphoreType.DMA((MESSAGES,)),
        pltpu.SemaphoreType.DMA((MESSAGES,)),
        pltpu.SemaphoreType.DMA((11,)),
    ]
    tokens = kept_half.shape[0]
    results = pl.pallas_call(
        kernel,
        out_shape=(
            jax.ShapeDtypeStruct((tokens, D), BF),
            jax.ShapeDtypeStruct((tokens, D), BF),
            jax.ShapeDtypeStruct((Q, 2 * F), BF),
            jax.ShapeDtypeStruct((Q, F), BF),
        ),
        in_specs=[hbm] * 7,
        out_specs=[hbm] * 4,
        scratch_shapes=scratch,
        compiler_params=pltpu.CompilerParams(
            collective_id=0, has_side_effects=True, vmem_limit_bytes=60 * 1024 * 1024
        ),
    )(kept_half, mixed_half, grad_kept, grad_mixed, gate_weight, up_weight, down_weight)
    *outs, grad_down = pl.pallas_call(
        hand_over,
        out_shape=(
            jax.ShapeDtypeStruct((tokens, D), BF),
            jax.ShapeDtypeStruct((tokens, D), BF),
            jax.ShapeDtypeStruct((1, Q, F), BF),
            jax.ShapeDtypeStruct((1, Q, F), BF),
            jax.ShapeDtypeStruct((Q, F), BF),
        ),
        in_specs=[hbm] * 4,
        out_specs=[hbm] * 5,
        scratch_shapes=[buf(tokens, D), buf(tokens, D), buf(Q, 2 * F), buf(Q, F), pltpu.SemaphoreType.DMA((9,))],
        compiler_params=pltpu.CompilerParams(vmem_limit_bytes=60 * 1024 * 1024),
    )(*results)
    return (*outs, grad_down.T[:, None, :])


def solution(mesh):
    in_specs = (
        P(("depth", "col"), "row"),
        P(("depth", "col"), "row"),
        P(("depth", "col"), "row"),
        P(("depth", "col"), "row"),
        P("row", "col"),
        P("row", "col"),
        P("col", "row"),
    )
    out_specs = (
        P(("depth", "col"), "row"),
        P(("depth", "col"), "row"),
        P("row", "depth", "col"),
        P("row", "depth", "col"),
        P("col", "row", "depth"),
    )
    return jax.shard_map(body, mesh=mesh, in_specs=in_specs, out_specs=out_specs, check_vma=False)
```

time: 447 us -> 98.8 us (0.22)
  waiting for transfers between devices: 345 us -> 0 us
  Pallas kernels: 0 us -> 97.9 us
  matrix products: 30.8 us -> 0 us
  blocking collectives: 29 us -> 0 us
  local copies, waits for them, and re-layouts: 20.9 us -> 0 us
  between operations: 14.2 us -> 0.8 us
  other arithmetic: 6.16 us -> 0 us
    reduce_scatter x3 -> x0, waiting for transfers between devices: 129 us -> none  [the longest x1 50.7 us: body(): lax.psum_scatter(jnp.concatenate([gate_part, up_part, back_part], axis=1)...]
    all_gather x2 -> x0, waiting for transfers between devices: 127 us -> none  [the longest x1 65.2 us: body(): lax.all_gather(kept_half, 'col', axis=0, tiled=True)]
    pallas_call x0 -> x2, Pallas kernels: none -> 97.9 us  [the longest x1 94.9 us: body(): pl.pallas_call(kernel, out_shape=(jax.ShapeDtypeStruct((tokens, D), BF),...]
    unnamed x9 -> x0, waiting for transfers between devices: 89 us -> none
    dot_general x9 -> x0, matrix products: 30.8 us -> none  [the longest x3 15.5 us: left_product(): lax.dot_general(left, right, (((0,), (0,)), ((), ())), preferred_element_...]
    all_gather x3 -> x0, blocking collectives: 29 us -> none  [the longest x1 9.69 us: body(): lax.all_gather(hidden, 'row', axis=0, tiled=True)]
    unnamed x30 -> x0, local copies, waits for them, and re-layouts: 20.9 us -> none
  transfers between devices with their start and end apart: 7 -> 0, of which waited for: 7 -> 0; matrix products, arithmetic and copies ran while one was open for 10% -> 0% of each run, Pallas kernels for 0% -> 0%
where the time goes in v2:
time: 98.8 us; the launch traced here: 98.7 us
  Pallas kernels  97.9 us (99%)
    pallas_call x1, Pallas kernels, body(): pl.pallas_call(kernel, out_shape=(jax.ShapeDtypeStruct((tokens, D), BF),...  94.9 us
    pallas_call x1, Pallas kernels, body(): pl.pallas_call(hand_over, out_shape=(jax.ShapeDtypeStruct((tokens, D), BF...  2.96 us

profile of v2, /device:TPU:1, one launch (start us, length us, event | category | flops | bytes accessed | tf_op | source)
XLA Modules:
  0.0 98.7 jit_solution(2714252305736266284)
XLA Ops:
  0.6 94.9 %shard_map.110 = (bf16[24,1792]{1,0:T(8,128)(2,1)}, bf16[24,1792]{1,0:T(8,128)(2,1)}, bf16[448,1792]{1,0:T(8,128)(2,1)}, bf16[448,896]{1,0:T(8,128)(2,1)}) custom-call(bf16[24,1792]{1,0:T(8,128)(2,1)} %kept_hbm.1, bf16[24,1792]{1,0:T(8,128)(2,1)} %mixed_hbm.1, bf16[24,1792]{1,0:T(8,128)(2,1)} %gkept_hbm.1, bf16[24,1792]{1,0:T(8,128)(2,1)} %gmixed_hbm.1, ...), custom_call_target="tpu_custom_call" | custom-call | tf_op jit(solution)/shard_map/pallas_call | solution.py:538
  95.6 3.0 %shard_map.111 = (bf16[24,1792]{1,0:T(8,128)(2,1)}, bf16[24,1792]{1,0:T(8,128)(2,1)}, bf16[1,448,896]{2,1,0:T(8,128)(2,1)}, bf16[1,448,896]{2,1,0:T(8,128)(2,1)}, bf16[448,896]{1,0:T(8,128)(2,1)}) custom-call(bf16[24,1792]{1,0:T(8,128)(2,1)} %get-tuple-element.14.restored, bf16[24,1792]{1,0:T(8,128)(2,1)} %get-tuple-element.15.grad_input, ...), custom_call_target="tpu_custom_call" | custom-call | tf_op jit(solution)/shard_map/pallas_call | solution.py:553

commit v3 on v0

v3 whole, which is shorter than its diff:
```python
import jax
import jax.numpy as jnp
from jax import lax
from jax.experimental import pallas as pl
from jax.experimental.pallas import tpu as pltpu
from jax.sharding import PartitionSpec as P

BF = jnp.bfloat16
F32 = jnp.float32
OFFSETS = (0, -1, 1, -2, 2, -3, 3, 4)
POS = {o: p for p, o in enumerate(OFFSETS)}
MESSAGES = 136
SENDS = 72
ORDER = (
    "start", "k1-", "k1+", "u0", "ua0", "wt5", "k0", "dnt", "sk0", "k2-0", "wt4", "k2-1", "k2+0", "wt0", "k2+1",
    "ua1", "gu0", "k3+0", "hg0", "k3-1", "u1+0", "sk1", "u1-0", "u1+1", "u1-1", "gu1", "ac0", "u2+0", "sk2", "u2-1",
    "hg1", "u2+1", "u2-0", "dh0", "h0s", "u3+0", "u3-1", "h0p1", "hb0", "ac1", "dh1", "h0p3", "hb1", "de0", "h1s",
    "br1", "wt1", "de1", "b1-0", "br0", "wt3", "b1+1", "b1+0", "wt6", "b1-1", "su0", "b2-0", "wt2", "b2+1", "g0s",
    "g1s", "b2-1", "b2+0", "g0r1", "bk1", "g1p1", "c1-0", "b3+1", "h1p1", "g0r3", "bk0", "hc1", "b3-1", "c1+1",
    "h1p3", "wg0", "c1-1", "c1+0", "g1p3", "su2", "c2-0", "gc1", "c2+1", "su1", "g0r2", "b3-0", "c2+0", "b3+0",
    "c2-1", "bl1", "wd0", "gc3", "c3-0", "c3+0", "c3+1", "hc2", "c3-1", "bl0", "gc2", "wg13", "cl0", "hc3", "bz",
    "cl1", "wg2", "wd13", "cz", "wd2",
)
RELAYED = ("g0", )


def dot(a, b):
    return jnp.dot(a, b, preferred_element_type=F32)


def tile(j, size):
    return pl.ds(pl.multiple_of(j * size, size), size)


class Message:
    def __init__(self, out, land):
        self.out, self.land, self.done, self.gone = out, land, False, False

    def start(self):
        self.out.start()
        return self

    def arrived(self):
        if self.done:
            return
        self.done = True
        self.land.wait_recv()

    def sent(self):
        if not self.gone:
            self.gone = True
            self.out.wait_send()


def kernel(
    kept_hbm, mixed_hbm, gkept_hbm, gmixed_hbm, gate_hbm, up_hbm, down_hbm,
    o_restored, o_grad_input, o_gate_up, o_down,
    kept, mixed, gkept, gmixed,
    w, dn, wt, dnt, xs, xr, xd, k, u, kt, ut, kta, uta,
    pg, pb, rg, rb, sg, sb, tg, tb, h, g,
    zb, zk, rbp, rbm, rkp, rkm, ys, yr, acc, acc_d,
    ss, rs, ls,
):
    d, r, c = lax.axis_index("depth"), lax.axis_index("row"), lax.axis_index("col")
    xh, co, xl, z = r // 2, r % 2, c // 8, c % 8
    F = w.shape[1] // 2
    D = w.shape[0]
    HD = D // 2
    T = 48
    Q = D // 4

    def at(depth=d, xhi=xh, core=co, xlo=xl, zz=z):
        return (depth, xhi * 2 + core, xlo * 8 + zz)

    z_next, z_prev = at(zz=(z + 1) % 8), at(zz=(z + 7) % 8)
    y_next, y_prev, y_far = (at(depth=(d + i) % 4) for i in (1, 3, 2))
    other_core, other_hi, other_lo = at(core=1 - co), at(xhi=1 - xh), at(xlo=1 - xl)
    z_next_lo, z_prev_lo = at(xlo=1 - xl, zz=(z + 1) % 8), at(xlo=1 - xl, zz=(z + 7) % 8)

    barrier = pltpu.get_barrier_semaphore()
    partners = (z_next, z_prev, z_next_lo, z_prev_lo, y_next, y_prev, y_far, other_core, other_hi, other_lo)
    for partner in partners:
        pl.semaphore_signal(barrier, inc=1, device_id=partner, device_id_type=pl.DeviceIdType.MESH)

    inputs = [
        pltpu.make_async_copy(src, dst, ls.at[3 + i])
        for i, (src, dst) in enumerate(
            ((kept_hbm, kept), (gmixed_hbm, gmixed), (mixed_hbm, mixed), (gkept_hbm, gkept))
        )
    ]
    for copy in inputs:
        copy.start()

    copies = [
        pltpu.make_async_copy(gate_hbm, w.at[:, pl.ds(0, F)], ls.at[0]),
        pltpu.make_async_copy(up_hbm, w.at[:, pl.ds(F, F)], ls.at[1]),
        pltpu.make_async_copy(down_hbm, dn, ls.at[2]),
    ]
    for copy in reversed(copies):
        copy.start()

    messages = []

    def message(src, dst, device, land=None):
        i = len(messages)
        if i >= SENDS:
            messages[i - SENDS].sent()
        sems = dict(
            send_sem=ss.at[i % SENDS], recv_sem=rs.at[i], device_id=device, device_id_type=pl.DeviceIdType.MESH
        )
        out = pltpu.make_async_remote_copy(src_ref=src, dst_ref=dst, **sems)
        into = out if land is None else pltpu.make_async_remote_copy(src_ref=src, dst_ref=land, **sems)
        m = Message(out, into)
        messages.append(m)
        return m

    flying = {}

    def send(name, src, dst, device, land=None):
        flying[name] = message(src, dst, device, land).start()

    def got(*names):
        for name in names:
            flying[name].arrived()

    loaded = set()

    def loads(*which):
        for i in which:
            if i not in loaded:
                loaded.add(i)
                copies[i].wait()

    finished = []

    def need(*names):
        assert all(name in finished for name in names), names

    pad = jnp.zeros((8, D), F32)
    for copy in inputs[:2]:
        copy.wait()
    own_k = kept[...].astype(F32)
    own_u = gmixed[...].astype(F32)
    xs[0] = jnp.concatenate([own_k, pad], axis=0).astype(BF)
    xs[1] = jnp.concatenate([own_u, pad], axis=0).astype(BF)

    pl.semaphore_wait(barrier, len(partners))

    def join(mine, theirs):
        first = jnp.where(xl == 0, mine, theirs)
        second = jnp.where(xl == 0, theirs, mine)
        return jnp.concatenate([first, second], axis=0).astype(BF)

    def part(ref, offset, f):
        return ref.at[pl.ds(T * POS[offset], T), pl.ds(HD * f, HD)]

    signs = {"+": (1, z_next, 0), "-": (-1, z_prev, 1)}
    rings = {"k": k, "u": u}

    def hop(a, h, s, f):
        sign, to, _ = signs[s]
        lands = -sign * h if h < 4 else 4
        send(f"{a}{h}{s}{f}", part(rings[a], -sign * (h - 1), f), part(rings[a], lands, f), to)

    ways = {1: (("+", 1),), 2: (("-", 1),), 3: (("+", 2),), 4: (("-", 2),), 5: (("+", 3),), 6: (("-", 3),)}

    def blocks(a, positions):
        need(f"{a}0")
        for p in positions:
            if p == 7:
                got(f"{a}4+0", f"{a}4-1")
            elif p > 0:
                ((s, h),) = ways[p]
                if a == "k" and h == 1:
                    need(f"k1{s}")
                else:
                    got(f"{a}{h}{s}0", f"{a}{h}{s}1")

    def turn_w(j):
        loads(0, 1)
        cols = pl.ds(256 * j, 256)
        wt[:, cols] = w[cols, :].T

    def turn_dn():
        loads(2)

        @pl.loop(0, 7)
        def _(j):
            dnt[tile(j, 256), :] = dn[:, tile(j, 256)].T

    def t_start():
        send("pk", xs.at[0], xr.at[0], other_lo)
        for to, name, slot, side in (
            (z_next, "kd+a", 0, 0), (z_prev, "kd-a", 1, 0), (z_next_lo, "kd+b", 0, 1), (z_prev_lo, "kd-b", 1, 1),
        ):
            send(name, xs.at[0], xd.at[slot, side], to)
        send("pu", xs.at[1], xr.at[1], other_lo)

    def t_own(a, i, own):
        got("p" + a)
        rings[a][pl.ds(0, T), :] = join(own, xr[i].astype(F32)[:24])

    def t_first(s):
        sign, _, i = signs[s]
        got(f"kd{s}a", f"kd{s}b")
        near, far = xd[i, 0].astype(F32)[:24], xd[i, 1].astype(F32)[:24]
        k[pl.ds(T * POS[-sign], T), :] = join(near, far)
        for f in (0, 1):
            hop("k", 2, s, f)

    def t_hop(a, h, s, f):
        got(f"{a}{h}{s}{f}")
        hop(a, h + 1, s, f)

    def t_spread(a, group):
        src, turned, gathered = {"k": (k, kt, kta), "u": (u, ut, uta)}[a]
        blocks(a, {0: (0, 1, 2), 1: (2, 3, 4, 5), 2: (5, 6, 7)}[group])

        @pl.loop(0, D // 256)
        def _(j):
            turned[group, tile(j, 256), :] = src[pl.ds(128 * group, 128), tile(j, 256)].T

        for slot, depth in ((1, (d + 1) % 4), (3, (d + 3) % 4), (2, (d + 2) % 4)):
            rows = pl.ds(pl.multiple_of(depth * Q, Q), Q)
            send(f"s{a}{group}{slot}", turned.at[group, rows], gathered.at[slot, group], at(depth=depth))

    def t_gate_up(half):
        blocks("k", range(4 * half, 4 * half + 4))
        loads(0, 1)
        pg[half] = dot(k[pl.ds(4 * T * half, 4 * T), :], w[...]).astype(BF).reshape(2, 2, T, 2 * F)
        send(f"cg{half}", pg.at[half, :, 1 - co], rg.at[half], other_core)

    def t_d_hidden(half):
        blocks("u", range(4 * half, 4 * half + 4))
        need("dnt")
        pb[half] = dot(u[pl.ds(4 * T * half, 4 * T), :], dnt[...]).astype(BF).reshape(2, 2, T, F)
        send(f"cb{half}", pb.at[half, :, 1 - co], rb.at[half], other_core)

    def t_hi(name, half):
        partial, received, summed, far = {"g": (pg, rg, sg, tg), "b": (pb, rb, sb, tb)}[name]
        got(f"c{name}{half}")
        there = 1 - xh
        summed[half] = (partial[half, there, co].astype(F32) + received[half, there].astype(F32)).astype(BF)
        send(f"h{name}{half}", summed.at[half], far.at[half], other_hi)

    def total(partial, received, far, half, lo, hi):
        cols = pl.ds(lo, hi - lo)
        return (
            partial[half, xh, co, :, cols].astype(F32)
            + received[half, xh, :, cols].astype(F32)
            + far[half, :, cols].astype(F32)
        )

    kept_values = {}

    def t_activate(half):
        got(f"hg{half}")
        gate = total(pg, rg, tg, half, 0, F)
        up = total(pg, rg, tg, half, F, 2 * F)
        logistic = jax.nn.sigmoid(gate)
        active = gate * logistic
        h[0, half, xh, co] = (active * up).astype(BF)
        kept_values[half] = up * logistic * (1.0 + gate * (1.0 - logistic)), active
        share("h", half)

    def t_deactivate(half):
        got(f"hb{half}")
        slope, active = kept_values[half]
        back = total(pb, rb, tb, half, 0, F)
        g[0, half, xh, co, :, pl.ds(0, F)] = (back * slope).astype(BF)
        g[0, half, xh, co, :, pl.ds(F, F)] = (back * active).astype(BF)
        share("g", half)

    shared = {"h": h, "g": g}

    def share(a, half):
        ref, n = shared[a], f"{a}{half}"
        own = ref.at[0, half, xh, co]
        send(f"{n}w", own, own, other_hi, ref.at[0, half, 1 - xh, co])
        send(f"{n}ca", own, own, other_core, ref.at[0, half, xh, 1 - co])
        send(f"{n}+", own, ref.at[1, half, xh, co], y_next)
        send(f"{n}-", own, ref.at[3, half, xh, co], y_prev)

    def t_second(a, half):
        ref, n = shared[a], f"{a}{half}"
        got(f"{n}w")
        far = ref.at[0, half, 1 - xh, co]
        send(f"{n}cb", far, far, other_core, ref.at[0, half, 1 - xh, 1 - co])
        if n not in RELAYED:
            send(f"{n}f+", far, ref.at[1, half, 1 - xh, co], y_next)
            send(f"{n}f-", far, ref.at[3, half, 1 - xh, co], y_prev)

    def t_pass(a, half, q):
        ref, n = shared[a], f"{a}{half}"
        if q == 1:
            got(f"{n}+")
            send(f"{n}l+", ref.at[1, half, xh, co], ref.at[2, half, xh, co], y_next)
        else:
            got(f"{n}f-")
            send(f"{n}l-", ref.at[3, half, 1 - xh, co], ref.at[2, half, 1 - xh, co], y_prev)

    def t_relay(a, half, q):
        ref, n = shared[a], f"{a}{half}"
        width = ref.shape[-1] // 2
        if q == 2:
            got(f"{n}l+", f"{n}l-")
        else:
            s, to, i = ("+", y_next, 0) if q == 1 else ("-", y_prev, 1)
            got(f"{n}{s}")
            cols = pl.ds(width * i, width)
            send(f"{n}l{s}", ref.at[q, half, xh, co, :, cols], ref.at[2, half, xh, co, :, cols], to)
        mine = ref.at[q, half, xh, co]
        send(f"{n}x{q}", mine, mine, other_hi, ref.at[q, half, 1 - xh, co])

    def t_to_core(a, q):
        for half in (0, 1):
            n = f"{a}{half}"
            if n in RELAYED:
                got(f"{n}x{q}")
            elif q == 2:
                got(f"{n}l+", f"{n}l-")
            else:
                s = "+" if q == 1 else "-"
                got(f"{n}{s}", f"{n}f{s}")
        ref = shared[a]
        mine = ref.at[q, :, :, co]
        send(f"{a}c{q}", mine, mine, other_core, ref.at[q, :, :, 1 - co])

    def here(a, half):
        got(f"{a}{half}w", f"{a}{half}ca", f"{a}{half}cb")

    sums = {"b": (zb, rbp, rbm, 0), "c": (zk, rkp, rkm, 1)}

    def ring_first(a):
        ref, plus, minus, _ = sums[a]
        send(f"{a}1+0", part(ref, 4, 0), plus.at[0, :, pl.ds(0, HD)], z_next)
        send(f"{a}1-1", part(ref, 4, 1), minus.at[0, :, pl.ds(HD, HD)], z_prev)

    def t_branch(half):
        here("h", half)
        loads(2)
        zb[pl.ds(4 * T * half, 4 * T), :] = dot(h[0, half].reshape(4 * T, F), dn[...]).astype(BF)
        if half == 1:
            ring_first("b")

    def t_grad_back(half):
        here("g", half)
        need(*(f"wt{j}" for j in range(7)))
        zk[pl.ds(4 * T * half, 4 * T), :] = dot(g[0, half].reshape(4 * T, 2 * F), wt[...]).astype(BF)
        if half == 1:
            ring_first("c")

    def t_sum(a, hop, s, f):
        ref, plus, minus, _ = sums[a]
        sign, to, _ = signs[s]
        received = plus if s == "+" else minus
        rows, cols = pl.ds(T * POS[sign * (4 - hop)], T), pl.ds(HD * f, HD)
        name = f"{a}{hop}{s}{f}"
        need({"b": "br1", "c": "bk1"}[a])
        if hop == 3 or (hop == 2 and s == "-"):
            need({"b": "br0", "c": "bk0"}[a])
        if name in flying:
            got(name)
            ref[rows, cols] = (ref[rows, cols].astype(F32) + received[hop - 1, :, cols].astype(F32)).astype(BF)
        else:
            assert hop == 1
        send(f"{a}{hop + 1}{s}{f}", ref.at[rows, cols], received.at[hop, :, cols], to)

    mine = {}

    def t_last(a, f):
        ref, plus, minus, i = sums[a]
        need({"b": "br0", "c": "bk0"}[a])
        cols = pl.ds(HD * f, HD)
        got(f"{a}4+{f}", f"{a}4-{f}")
        whole = ref[pl.ds(0, T), cols].astype(F32) + plus[3, :, cols].astype(F32) + minus[3, :, cols].astype(F32)
        mine[a, f] = jnp.where(xl == 0, whole[:24], whole[24:])
        theirs = jnp.where(xl == 0, whole[24:], whole[:24])
        ys[i, f] = jnp.concatenate([theirs, pad[:, :HD]], axis=0).astype(BF)
        send(f"{a}e{f}", ys.at[i, f], yr.at[i, f], other_lo)

    def t_result(a, out, base, sign):
        i = sums[a][3]
        inputs[2 + i].wait()
        for f in (0, 1):
            cols = pl.ds(HD * f, HD)
            got(f"{a}e{f}")
            whole = mine[a, f] + yr[i, f].astype(F32)[:24]
            out[:, cols] = (base[:, cols].astype(F32) + sign * whole).astype(BF)

    own_rows = pl.ds(pl.multiple_of(d * Q, Q), Q)

    def turned(q, mine, gathered):
        if q == 0:
            return [mine[i, own_rows, :] for i in range(3)]
        return [gathered[q, i] for i in range(3)]

    def grads_gate_up(qs, first=False, end=False):
        lhs = jnp.concatenate([x for q in qs for x in turned(q, kt, kta)], axis=1)
        rhs = jnp.concatenate([g[q].reshape(8 * T, 2 * F) for q in qs], axis=0)
        term = dot(lhs, rhs)
        if not first:
            term = term + acc[...]
        if end:
            o_gate_up[...] = term.astype(BF)
        else:
            acc[...] = term

    def grads_down(qs, first=False, end=False):
        lhs = jnp.concatenate([x for q in qs for x in turned(q, ut, uta)], axis=1)
        rhs = jnp.concatenate([h[q].reshape(8 * T, F) for q in qs], axis=0)
        term = dot(lhs, rhs)
        if not first:
            term = term + acc_d[...]
        if end:
            o_down[...] = term.astype(BF)
        else:
            acc_d[...] = term

    def t_grads(a, qs):
        small = a == "h"
        turns, fn = ("su", grads_down) if small else ("sk", grads_gate_up)
        first, end = 0 in qs, 2 in qs
        for q in qs:
            if q == 0:
                need(*(f"{turns}{i}" for i in range(3)))
                here(a, 0)
                here(a, 1)
            else:
                got(f"{a}c{q}", *(f"{turns}{i}{q}" for i in range(3)))
                for half in (0, 1):
                    n = f"{a}{half}"
                    if n in RELAYED:
                        got(f"{n}x{q}")
        if not first:
            need("wd0" if small else "wg0")
        if end:
            need("wd13" if small else "wg13")
        fn(qs, first=first, end=end)

    tasks = {"start": t_start, "dnt": turn_dn}
    tasks |= {f"wt{j}": (turn_w, j) for j in range(7)}
    tasks |= {"k0": (t_own, "k", 0, own_k), "u0": (t_own, "u", 1, own_u)}
    tasks |= {"k1+": (t_first, "+"), "k1-": (t_first, "-")}

    def t_start_u(f):
        need("u0")
        for s in "+-":
            hop("u", 1, s, f)

    for i in (0, 1):
        tasks |= {
            f"ua{i}": (t_start_u, i),
            f"gu{i}": (t_gate_up, i), f"dh{i}": (t_d_hidden, i),
            f"hg{i}": (t_hi, "g", i), f"hb{i}": (t_hi, "b", i),
            f"ac{i}": (t_activate, i), f"de{i}": (t_deactivate, i),
            f"br{i}": (t_branch, i), f"bk{i}": (t_grad_back, i),
            f"bl{i}": (t_last, "b", i), f"cl{i}": (t_last, "c", i),
        }
        for a in "hg":
            n = f"{a}{i}"
            tasks |= {f"{n}s": (t_second, a, i)}
            if n in RELAYED:
                tasks |= {f"{n}r{q}": (t_relay, a, i, q) for q in (1, 3, 2)}
            else:
                tasks |= {f"{n}p{q}": (t_pass, a, i, q) for q in (1, 3)}
    tasks |= {f"s{a}{i}": (t_spread, a, i) for a in "ku" for i in range(3)}
    tasks |= {f"{a}c{q}": (t_to_core, a, q) for a in "hg" for q in (1, 3, 2)}
    for s in "+-":
        for f in (0, 1):
            for hops in (1, 2, 3):
                ends = hops < 3 or (s, f) in (("+", 0), ("-", 1))
                if ends and hops > 1:
                    tasks[f"k{hops}{s}{f}"] = (t_hop, "k", hops, s, f)
                if ends:
                    tasks[f"u{hops}{s}{f}"] = (t_hop, "u", hops, s, f)
                for a in "bc":
                    tasks[f"{a}{hops}{s}{f}"] = (t_sum, a, hops, s, f)
    tasks |= {"wd0": (t_grads, "h", (0,)), "wd13": (t_grads, "h", (1, 3)), "wd2": (t_grads, "h", (2,))}
    tasks |= {"wg0": (t_grads, "g", (0,)), "wg13": (t_grads, "g", (1, 3)), "wg2": (t_grads, "g", (2,))}
    tasks |= {"bz": (t_result, "b", o_restored, mixed, -1.0), "cz": (t_result, "c", o_grad_input, gkept, 1.0)}

    assert len(ORDER) == len(tasks) and set(ORDER) == set(tasks)
    for name in ORDER:
        task = tasks[name]
        if callable(task):
            task()
        else:
            task[0](*task[1:])
        finished.append(name)
    for m in messages:
        m.arrived()
        m.sent()
    assert len(messages) <= MESSAGES


def hand_over(restored, grad_input, gate_up, down, o_restored, o_grad_input, o_gate, o_up, o_down, sems):
    F = o_gate.shape[2]
    pairs = (
        (gate_up.at[:, pl.ds(0, F)], o_gate.at[0]),
        (gate_up.at[:, pl.ds(F, F)], o_up.at[0]),
        (down, o_down),
        (restored, o_restored),
        (grad_input, o_grad_input),
    )
    copies = [pltpu.make_async_copy(src, dst, sems.at[i]) for i, (src, dst) in enumerate(pairs)]
    for copy in copies:
        copy.start()
    for copy in copies:
        copy.wait()


def body(kept_half, mixed_half, grad_kept, grad_mixed, gate_weight, up_weight, down_weight):
    D, F = gate_weight.shape
    Q = D // 4
    T = 48
    hbm = pl.BlockSpec(memory_space=pl.ANY)
    vmem = pl.BlockSpec(memory_space=pltpu.VMEM)

    def buf(*shape, dtype=BF):
        return pltpu.VMEM(shape, dtype)

    scratch = [
        *[buf(24, D)] * 4,
        buf(D, 2 * F), buf(F, D), buf(2 * F, D), buf(D, F),
        buf(2, 32, D), buf(2, 32, D), buf(2, 2, 32, D),
        buf(384, D), buf(384, D),
        buf(3, D, 128), buf(3, D, 128),
        buf(4, 3, Q, 128), buf(4, 3, Q, 128),
        buf(2, 2, 2, T, 2 * F), buf(2, 2, 2, T, F),
        buf(2, 2, T, 2 * F), buf(2, 2, T, F),
        buf(2, T, 2 * F), buf(2, T, F), buf(2, T, 2 * F), buf(2, T, F),
        buf(4, 2, 2, 2, T, F), buf(4, 2, 2, 2, T, 2 * F),
        buf(384, D), buf(384, D),
        buf(4, T, D), buf(4, T, D), buf(4, T, D), buf(4, T, D),
        buf(2, 2, 32, D // 2), buf(2, 2, 32, D // 2),
        buf(Q, 2 * F, dtype=F32), buf(Q, F, dtype=F32),
        pltpu.SemaphoreType.DMA((SENDS,)),
        pltpu.SemaphoreType.DMA((MESSAGES,)),
        pltpu.SemaphoreType.DMA((7,)),
    ]
    tokens = kept_half.shape[0]
    results = pl.pallas_call(
        kernel,
        out_shape=(buf(tokens, D), buf(tokens, D), buf(Q, 2 * F), buf(Q, F)),
        in_specs=[hbm] * 7,
        out_specs=[vmem] * 4,
        scratch_shapes=scratch,
        compiler_params=pltpu.CompilerParams(
            collective_id=0, has_side_effects=True, vmem_limit_bytes=57 * 1024 * 1024
        ),
    )(kept_half, mixed_half, grad_kept, grad_mixed, gate_weight, up_weight, down_weight)
    *outs, grad_down = pl.pallas_call(
        hand_over,
        out_shape=(
            jax.ShapeDtypeStruct((tokens, D), BF),
            jax.ShapeDtypeStruct((tokens, D), BF),
            jax.ShapeDtypeStruct((1, Q, F), BF),
            jax.ShapeDtypeStruct((1, Q, F), BF),
            jax.ShapeDtypeStruct((Q, F), BF),
        ),
        in_specs=[vmem] * 4,
        out_specs=[hbm] * 5,
        scratch_shapes=[pltpu.SemaphoreType.DMA((5,))],
        compiler_params=pltpu.CompilerParams(vmem_limit_bytes=4 * 1024 * 1024),
    )(*results)
    return (*outs, grad_down.T[:, None, :])


def solution(mesh):
    in_specs = (
        P(("depth", "col"), "row"),
        P(("depth", "col"), "row"),
        P(("depth", "col"), "row"),
        P(("depth", "col"), "row"),
        P("row", "col"),
        P("row", "col"),
        P("col", "row"),
    )
    out_specs = (
        P(("depth", "col"), "row"),
        P(("depth", "col"), "row"),
        P("row", "depth", "col"),
        P("row", "depth", "col"),
        P("col", "row", "depth"),
    )
    return jax.shard_map(body, mesh=mesh, in_specs=in_specs, out_specs=out_specs, check_vma=False)
```

time: 447 us -> 89 us (0.20)
  waiting for transfers between devices: 345 us -> 0 us
  Pallas kernels: 0 us -> 88.1 us
  matrix products: 30.8 us -> 0 us
  blocking collectives: 29 us -> 0 us
  local copies, waits for them, and re-layouts: 20.9 us -> 0 us
  between operations: 14.2 us -> 0.8 us
  other arithmetic: 6.16 us -> 0 us
    reduce_scatter x3 -> x0, waiting for transfers between devices: 129 us -> none  [the longest x1 50.7 us: body(): lax.psum_scatter(jnp.concatenate([gate_part, up_part, back_part], axis=1)...]
    all_gather x2 -> x0, waiting for transfers between devices: 127 us -> none  [the longest x1 65.2 us: body(): lax.all_gather(kept_half, 'col', axis=0, tiled=True)]
    unnamed x9 -> x0, waiting for transfers between devices: 89 us -> none
    pallas_call x0 -> x2, Pallas kernels: none -> 88.1 us  [the longest x1 86.6 us: body(): pl.pallas_call(kernel, out_shape=(buf(tokens, D), buf(tokens, D), buf(Q,...]
    dot_general x9 -> x0, matrix products: 30.8 us -> none  [the longest x3 15.5 us: left_product(): lax.dot_general(left, right, (((0,), (0,)), ((), ())), preferred_element_...]
    all_gather x3 -> x0, blocking collectives: 29 us -> none  [the longest x1 9.69 us: body(): lax.all_gather(hidden, 'row', axis=0, tiled=True)]
    unnamed x30 -> x0, local copies, waits for them, and re-layouts: 20.9 us -> none
  transfers between devices with their start and end apart: 7 -> 0, of which waited for: 7 -> 0; matrix products, arithmetic and copies ran while one was open for 10% -> 0% of each run, Pallas kernels for 0% -> 0%
where the time goes in v3:
time: 89 us; the launch traced here: 88.9 us
  Pallas kernels  88.1 us (99%)
    pallas_call x1, Pallas kernels, body(): pl.pallas_call(kernel, out_shape=(buf(tokens, D), buf(tokens, D), buf(Q,...  86.6 us

profile of v3, /device:TPU:1, one launch (start us, length us, event | category | flops | bytes accessed | tf_op | source)
XLA Modules:
  0.0 88.9 jit_solution(13177965156375409558)
XLA Ops:
  0.6 86.6 %shard_map.110 = (bf16[24,1792]{1,0:T(8,128)(2,1)S(1)}, bf16[24,1792]{1,0:T(8,128)(2,1)S(1)}, bf16[448,1792]{1,0:T(8,128)(2,1)S(1)}, bf16[448,896]{1,0:T(8,128)(2,1)S(1)}) custom-call(bf16[24,1792]{1,0:T(8,128)(2,1)} %kept_hbm.1, bf16[24,1792]{1,0:T(8,128)(2,1)} %mixed_hbm.1, bf16[24,1792]{1,0:T(8,128)(2,1)} %gkept_hbm.1, bf16[24,1792]{1,0:T(8,128)(2,1)} %gmixed_hbm.1, ...), custom_call_target="tpu_custom_call" | custom-call | tf_op jit(solution)/shard_map/pallas_call | solution.py:543
  87.3 1.5 %shard_map.111 = (bf16[24,1792]{1,0:T(8,128)(2,1)}, bf16[24,1792]{1,0:T(8,128)(2,1)}, bf16[1,448,896]{2,1,0:T(8,128)(2,1)}, bf16[1,448,896]{2,1,0:T(8,128)(2,1)}, bf16[448,896]{1,0:T(8,128)(2,1)}) custom-call(bf16[24,1792]{1,0:T(8,128)(2,1)S(1)} %get-tuple-element.14.restored, bf16[24,1792]{1,0:T(8,128)(2,1)S(1)} %get-tuple-element.15.grad_input, ...), custom_call_target="tpu_custom_call" | custom-call | tf_op jit(solution)/shard_map/pallas_call | solution.py:553

commit v4 on v3

--- a/solution.py
+++ b/solution.py
@@ -9,17 +9,16 @@
 F32 = jnp.float32
 OFFSETS = (0, -1, 1, -2, 2, -3, 3, 4)
 POS = {o: p for p, o in enumerate(OFFSETS)}
-MESSAGES = 136
-SENDS = 72
+MESSAGES = 132
+SENDS = 32
 ORDER = (
-    "start", "k1-", "k1+", "u0", "ua0", "wt5", "k0", "dnt", "sk0", "k2-0", "wt4", "k2-1", "k2+0", "wt0", "k2+1",
-    "ua1", "gu0", "k3+0", "hg0", "k3-1", "u1+0", "sk1", "u1-0", "u1+1", "u1-1", "gu1", "ac0", "u2+0", "sk2", "u2-1",
-    "hg1", "u2+1", "u2-0", "dh0", "h0s", "u3+0", "u3-1", "h0p1", "hb0", "ac1", "dh1", "h0p3", "hb1", "de0", "h1s",
-    "br1", "wt1", "de1", "b1-0", "br0", "wt3", "b1+1", "b1+0", "wt6", "b1-1", "su0", "b2-0", "wt2", "b2+1", "g0s",
-    "g1s", "b2-1", "b2+0", "g0r1", "bk1", "g1p1", "c1-0", "b3+1", "h1p1", "g0r3", "bk0", "hc1", "b3-1", "c1+1",
-    "h1p3", "wg0", "c1-1", "c1+0", "g1p3", "su2", "c2-0", "gc1", "c2+1", "su1", "g0r2", "b3-0", "c2+0", "b3+0",
-    "c2-1", "bl1", "wd0", "gc3", "c3-0", "c3+0", "c3+1", "hc2", "c3-1", "bl0", "gc2", "wg13", "cl0", "hc3", "bz",
-    "cl1", "wg2", "wd13", "cz", "wd2",
+    "start", "wt4", "dnt", "wt5", "k1+", "k1-", "k0", "sk0", "wt0", "wt3", "k2+0", "u0", "k2-0", "k2+1", "k2-1",
+    "ua1", "gu0", "ua0", "sk1", "k3+0", "hg0", "k3-1", "wt6", "u1+0", "u1-1", "su0", "u1-0", "u1+1", "gu1", "u2+0",
+    "u2-1", "ac0", "sk2", "u2-0", "u2+1", "hg1", "dh0", "u3-1", "u3+0", "h0s", "wt1", "hb0", "br0", "dh1", "ac1",
+    "wt2", "hb1", "de0", "h1s", "br1", "b1+1", "de1", "b1-0", "h0p3", "bp", "b1-1", "b1+0", "hc3", "b2-0", "g0s",
+    "h0p1", "g0r1", "g1s", "b2+1", "h1p1", "g0r3", "b2-1", "b2+0", "bk1", "hc1", "g1p1", "c1+1", "c1-0", "bk0",
+    "h1p3", "cp", "wg0", "c1+0", "g1p3", "c1-1", "c2-0", "g0r2", "gc3", "c2+1", "su1", "c2+0", "gc1", "c2-1", "b3-",
+    "hc2", "b3+", "su2", "wd0", "c3+", "gc2", "c3-", "wg13", "wg2", "bz", "wd13", "cz", "wd2",
 )
 RELAYED = ("g0", )
 
@@ -136,13 +135,19 @@
     def need(*names):
         assert all(name in finished for name in names), names
 
-    pad = jnp.zeros((8, D), F32)
+    def pack(x):
+        return jnp.concatenate([x[:, :HD], x[:, HD:]], axis=0).astype(BF)
+
+    def unpack(x):
+        x = x.astype(F32)
+        return jnp.concatenate([x[:24], x[24:]], axis=1)
+
     for copy in inputs[:2]:
         copy.wait()
     own_k = kept[...].astype(F32)
     own_u = gmixed[...].astype(F32)
-    xs[0] = jnp.concatenate([own_k, pad], axis=0).astype(BF)
-    xs[1] = jnp.concatenate([own_u, pad], axis=0).astype(BF)
+    xs[0] = pack(own_k)
+    xs[1] = pack(own_u)
 
     pl.semaphore_wait(barrier, len(partners))
 
@@ -189,21 +194,21 @@
             dnt[tile(j, 256), :] = dn[:, tile(j, 256)].T
 
     def t_start():
-        send("pk", xs.at[0], xr.at[0], other_lo)
         for to, name, slot, side in (
             (z_next, "kd+a", 0, 0), (z_prev, "kd-a", 1, 0), (z_next_lo, "kd+b", 0, 1), (z_prev_lo, "kd-b", 1, 1),
         ):
             send(name, xs.at[0], xd.at[slot, side], to)
+        send("pk", xs.at[0], xr.at[0], other_lo)
         send("pu", xs.at[1], xr.at[1], other_lo)
 
     def t_own(a, i, own):
         got("p" + a)
-        rings[a][pl.ds(0, T), :] = join(own, xr[i].astype(F32)[:24])
+        rings[a][pl.ds(0, T), :] = join(own, unpack(xr[i]))
 
     def t_first(s):
         sign, _, i = signs[s]
         got(f"kd{s}a", f"kd{s}b")
-        near, far = xd[i, 0].astype(F32)[:24], xd[i, 1].astype(F32)[:24]
+        near, far = unpack(xd[i, 0]), unpack(xd[i, 1])
         k[pl.ds(T * POS[-sign], T), :] = join(near, far)
         for f in (0, 1):
             hop("k", 2, s, f)
@@ -357,7 +362,7 @@
         rows, cols = pl.ds(T * POS[sign * (4 - hop)], T), pl.ds(HD * f, HD)
         name = f"{a}{hop}{s}{f}"
         need({"b": "br1", "c": "bk1"}[a])
-        if hop == 3 or (hop == 2 and s == "-"):
+        if hop == 2 and s == "-":
             need({"b": "br0", "c": "bk0"}[a])
         if name in flying:
             got(name)
@@ -366,27 +371,36 @@
             assert hop == 1
         send(f"{a}{hop + 1}{s}{f}", ref.at[rows, cols], received.at[hop, :, cols], to)
 
-    mine = {}
-
-    def t_last(a, f):
+    def rows_for(x, here):
+        return jnp.where((xl == 0) == here, x[:24], x[24:])
+
+    def t_pair(a):
+        ref, _, _, i = sums[a]
+        need({"b": "br0", "c": "bk0"}[a])
+        ys[i, 0] = pack(rows_for(ref[pl.ds(0, T), :].astype(F32), False))
+        send(f"{a}p", ys.at[i, 0], yr.at[i, 0], other_lo)
+
+    def t_sum_last(a, s):
         ref, plus, minus, i = sums[a]
+        sign, to, side = signs[s]
         need({"b": "br0", "c": "bk0"}[a])
-        cols = pl.ds(HD * f, HD)
-        got(f"{a}4+{f}", f"{a}4-{f}")
-        whole = ref[pl.ds(0, T), cols].astype(F32) + plus[3, :, cols].astype(F32) + minus[3, :, cols].astype(F32)
-        mine[a, f] = jnp.where(xl == 0, whole[:24], whole[24:])
-        theirs = jnp.where(xl == 0, whole[24:], whole[:24])
-        ys[i, f] = jnp.concatenate([theirs, pad[:, :HD]], axis=0).astype(BF)
-        send(f"{a}e{f}", ys.at[i, f], yr.at[i, f], other_lo)
+        got(f"{a}3{s}0", f"{a}3{s}1")
+        received = plus if s == "+" else minus
+        whole = ref[pl.ds(T * POS[sign], T), :].astype(F32) + received[2].astype(F32)
+        to_lo = z_next_lo if s == "+" else z_prev_lo
+        ys[i, 1 + 2 * side] = pack(rows_for(whole, False))
+        send(f"{a}4{s}b", ys.at[i, 1 + 2 * side], yr.at[i, 1 + 2 * side], to_lo)
+        ys[i, 2 + 2 * side] = pack(rows_for(whole, True))
+        send(f"{a}4{s}a", ys.at[i, 2 + 2 * side], yr.at[i, 2 + 2 * side], to)
 
     def t_result(a, out, base, sign):
-        i = sums[a][3]
+        ref, _, _, i = sums[a]
         inputs[2 + i].wait()
-        for f in (0, 1):
-            cols = pl.ds(HD * f, HD)
-            got(f"{a}e{f}")
-            whole = mine[a, f] + yr[i, f].astype(F32)[:24]
-            out[:, cols] = (base[:, cols].astype(F32) + sign * whole).astype(BF)
+        got(f"{a}p", *(f"{a}4{s}{x}" for s in "+-" for x in "ab"))
+        whole = rows_for(ref[pl.ds(0, T), :].astype(F32), True)
+        for part_of in range(5):
+            whole = whole + unpack(yr[i, part_of])
+        out[...] = (base[...].astype(F32) + sign * whole).astype(BF)
 
     own_rows = pl.ds(pl.multiple_of(d * Q, Q), Q)
 
@@ -455,7 +469,6 @@
             f"hg{i}": (t_hi, "g", i), f"hb{i}": (t_hi, "b", i),
             f"ac{i}": (t_activate, i), f"de{i}": (t_deactivate, i),
             f"br{i}": (t_branch, i), f"bk{i}": (t_grad_back, i),
-            f"bl{i}": (t_last, "b", i), f"cl{i}": (t_last, "c", i),
         }
         for a in "hg":
             n = f"{a}{i}"
@@ -474,8 +487,11 @@
                     tasks[f"k{hops}{s}{f}"] = (t_hop, "k", hops, s, f)
                 if ends:
                     tasks[f"u{hops}{s}{f}"] = (t_hop, "u", hops, s, f)
-                for a in "bc":
-                    tasks[f"{a}{hops}{s}{f}"] = (t_sum, a, hops, s, f)
+                if hops < 3:
+                    for a in "bc":
+                        tasks[f"{a}{hops}{s}{f}"] = (t_sum, a, hops, s, f)
+    for a in "bc":
+        tasks |= {f"{a}p": (t_pair, a), f"{a}3+": (t_sum_last, a, "+"), f"{a}3-": (t_sum_last, a, "-")}
     tasks |= {"wd0": (t_grads, "h", (0,)), "wd13": (t_grads, "h", (1, 3)), "wd2": (t_grads, "h", (2,))}
     tasks |= {"wg0": (t_grads, "g", (0,)), "wg13": (t_grads, "g", (1, 3)), "wg2": (t_grads, "g", (2,))}
     tasks |= {"bz": (t_result, "b", o_restored, mixed, -1.0), "cz": (t_result, "c", o_grad_input, gkept, 1.0)}
@@ -514,6 +530,7 @@
     D, F = gate_weight.shape
     Q = D // 4
     T = 48
+    tokens = kept_half.shape[0]
     hbm = pl.BlockSpec(memory_space=pl.ANY)
     vmem = pl.BlockSpec(memory_space=pltpu.VMEM)
 
@@ -523,7 +540,7 @@
     scratch = [
         *[buf(24, D)] * 4,
         buf(D, 2 * F), buf(F, D), buf(2 * F, D), buf(D, F),
-        buf(2, 32, D), buf(2, 32, D), buf(2, 2, 32, D),
+        *[buf(2, 2 * tokens, D // 2)] * 2, buf(2, 2, 2 * tokens, D // 2),
         buf(384, D), buf(384, D),
         buf(3, D, 128), buf(3, D, 128),
         buf(4, 3, Q, 128), buf(4, 3, Q, 128),
@@ -532,14 +549,13 @@
         buf(2, T, 2 * F), buf(2, T, F), buf(2, T, 2 * F), buf(2, T, F),
         buf(4, 2, 2, 2, T, F), buf(4, 2, 2, 2, T, 2 * F),
         buf(384, D), buf(384, D),
-        buf(4, T, D), buf(4, T, D), buf(4, T, D), buf(4, T, D),
-        buf(2, 2, 32, D // 2), buf(2, 2, 32, D // 2),
+        *[buf(3, T, D)] * 4,
+        *[buf(2, 5, 2 * tokens, D // 2)] * 2,
         buf(Q, 2 * F, dtype=F32), buf(Q, F, dtype=F32),
         pltpu.SemaphoreType.DMA((SENDS,)),
         pltpu.SemaphoreType.DMA((MESSAGES,)),
         pltpu.SemaphoreType.DMA((7,)),
     ]
-    tokens = kept_half.shape[0]
     results = pl.pallas_call(
         kernel,
         out_shape=(buf(tokens, D), buf(tokens, D), buf(Q, 2 * F), buf(Q, F)),

time: 89 us -> 86.4 us (0.971)
  Pallas kernels: 88.1 us -> 85.3 us
    pallas_call x1, Pallas kernels: 86.6 us -> 83.8 us  [body(): pl.pallas_call(kernel, out_shape=(buf(tokens, D), buf(tokens, D), buf(Q,...]
where the time goes in v4:
time: 86.4 us; the launch traced here: 86.1 us
  Pallas kernels  85.3 us (99%)
    pallas_call x1, Pallas kernels, body(): pl.pallas_call(kernel, out_shape=(buf(tokens, D), buf(tokens, D), buf(Q,...  83.8 us

profile of v4, /device:TPU:1, one launch (start us, length us, event | category | flops | bytes accessed | tf_op | source)
XLA Modules:
  0.0 86.1 jit_solution(12056458239234432869)
XLA Ops:
  0.6 83.8 %shard_map.110 = (bf16[24,1792]{1,0:T(8,128)(2,1)S(1)}, bf16[24,1792]{1,0:T(8,128)(2,1)S(1)}, bf16[448,1792]{1,0:T(8,128)(2,1)S(1)}, bf16[448,896]{1,0:T(8,128)(2,1)S(1)}) custom-call(bf16[24,1792]{1,0:T(8,128)(2,1)} %kept_hbm.1, bf16[24,1792]{1,0:T(8,128)(2,1)} %mixed_hbm.1, bf16[24,1792]{1,0:T(8,128)(2,1)} %gkept_hbm.1, bf16[24,1792]{1,0:T(8,128)(2,1)} %gmixed_hbm.1, ...), custom_call_target="tpu_custom_call" | custom-call | tf_op jit(solution)/shard_map/pallas_call | solution.py:559
  84.4 1.5 %shard_map.111 = (bf16[24,1792]{1,0:T(8,128)(2,1)}, bf16[24,1792]{1,0:T(8,128)(2,1)}, bf16[1,448,896]{2,1,0:T(8,128)(2,1)}, bf16[1,448,896]{2,1,0:T(8,128)(2,1)}, bf16[448,896]{1,0:T(8,128)(2,1)}) custom-call(bf16[24,1792]{1,0:T(8,128)(2,1)S(1)} %get-tuple-element.14.restored, bf16[24,1792]{1,0:T(8,128)(2,1)S(1)} %get-tuple-element.15.grad_input, ...), custom_call_target="tpu_custom_call" | custom-call | tf_op jit(solution)/shard_map/pallas_call | solution.py:569

commit v5 on v3

--- a/solution.py
+++ b/solution.py
@@ -10,18 +10,18 @@
 OFFSETS = (0, -1, 1, -2, 2, -3, 3, 4)
 POS = {o: p for p, o in enumerate(OFFSETS)}
 MESSAGES = 136
-SENDS = 72
+SENDS = 24
 ORDER = (
-    "start", "k1-", "k1+", "u0", "ua0", "wt5", "k0", "dnt", "sk0", "k2-0", "wt4", "k2-1", "k2+0", "wt0", "k2+1",
-    "ua1", "gu0", "k3+0", "hg0", "k3-1", "u1+0", "sk1", "u1-0", "u1+1", "u1-1", "gu1", "ac0", "u2+0", "sk2", "u2-1",
-    "hg1", "u2+1", "u2-0", "dh0", "h0s", "u3+0", "u3-1", "h0p1", "hb0", "ac1", "dh1", "h0p3", "hb1", "de0", "h1s",
-    "br1", "wt1", "de1", "b1-0", "br0", "wt3", "b1+1", "b1+0", "wt6", "b1-1", "su0", "b2-0", "wt2", "b2+1", "g0s",
-    "g1s", "b2-1", "b2+0", "g0r1", "bk1", "g1p1", "c1-0", "b3+1", "h1p1", "g0r3", "bk0", "hc1", "b3-1", "c1+1",
-    "h1p3", "wg0", "c1-1", "c1+0", "g1p3", "su2", "c2-0", "gc1", "c2+1", "su1", "g0r2", "b3-0", "c2+0", "b3+0",
-    "c2-1", "bl1", "wd0", "gc3", "c3-0", "c3+0", "c3+1", "hc2", "c3-1", "bl0", "gc2", "wg13", "cl0", "hc3", "bz",
-    "cl1", "wg2", "wd13", "cz", "wd2",
+    "start", "dnt", "wt4", "k1+", "k1-", "k0", "wt1", "sk0", "k2+0", "k2-0", "u0", "wt0", "k2+1", "ua0", "gu0",
+    "k2-1", "wt3", "ua1", "wt2", "sk1", "hg0", "k3+0", "wt5", "k3-1", "u1+0", "u1-1", "su0", "u1-0", "u1+1", "gu1",
+    "u2+0", "u2-1", "ac0", "u2+1", "u2-0", "hg1", "dh0", "u3+0", "u3-1", "sk2", "hb0", "h0s", "dh1", "ac1", "hb1",
+    "br0", "de0", "h1s", "br1", "b1-0", "de1", "b1+1", "wt6", "g0s", "g0r1", "g0r3", "b1+0", "b1-1", "b2+1", "b2-0",
+    "g1s", "h0r1", "g1p1", "h0r3", "b2-1", "b2+0", "bk1", "c1+1", "su2", "c1-0", "bk0", "b3-1", "c1+0", "g0r2",
+    "gc1", "g1p3", "b3+1", "c1-1", "wg0", "h0r2", "c2-0", "h1p3", "h1p1", "gc3", "c2+0", "c2+1", "b3+0", "b3-0",
+    "hc3", "su1", "c2-1", "wg13", "c3+0", "bl1", "c3-0", "wd0", "c3+1", "hc1", "c3-1", "gc2", "hc2", "bl0", "cl0",
+    "wd13", "cl1", "wg2", "wd2", "bz", "cz",
 )
-RELAYED = ("g0", )
+RELAYED = ("h0", "g0", )
 
 
 def dot(a, b):
@@ -136,13 +136,21 @@
     def need(*names):
         assert all(name in finished for name in names), names
 
-    pad = jnp.zeros((8, D), F32)
+    pad = jnp.zeros((8, HD), F32)
+
+    def pack(x):
+        return jnp.concatenate([x[:, :HD], x[:, HD:]], axis=0).astype(BF)
+
+    def unpack(x):
+        x = x.astype(F32)
+        return jnp.concatenate([x[:24], x[24:]], axis=1)
+
     for copy in inputs[:2]:
         copy.wait()
     own_k = kept[...].astype(F32)
     own_u = gmixed[...].astype(F32)
-    xs[0] = jnp.concatenate([own_k, pad], axis=0).astype(BF)
-    xs[1] = jnp.concatenate([own_u, pad], axis=0).astype(BF)
+    xs[0] = pack(own_k)
+    xs[1] = pack(own_u)
 
     pl.semaphore_wait(barrier, len(partners))
 
@@ -189,21 +197,21 @@
             dnt[tile(j, 256), :] = dn[:, tile(j, 256)].T
 
     def t_start():
-        send("pk", xs.at[0], xr.at[0], other_lo)
         for to, name, slot, side in (
             (z_next, "kd+a", 0, 0), (z_prev, "kd-a", 1, 0), (z_next_lo, "kd+b", 0, 1), (z_prev_lo, "kd-b", 1, 1),
         ):
             send(name, xs.at[0], xd.at[slot, side], to)
+        send("pk", xs.at[0], xr.at[0], other_lo)
         send("pu", xs.at[1], xr.at[1], other_lo)
 
     def t_own(a, i, own):
         got("p" + a)
-        rings[a][pl.ds(0, T), :] = join(own, xr[i].astype(F32)[:24])
+        rings[a][pl.ds(0, T), :] = join(own, unpack(xr[i]))
 
     def t_first(s):
         sign, _, i = signs[s]
         got(f"kd{s}a", f"kd{s}b")
-        near, far = xd[i, 0].astype(F32)[:24], xd[i, 1].astype(F32)[:24]
+        near, far = unpack(xd[i, 0]), unpack(xd[i, 1])
         k[pl.ds(T * POS[-sign], T), :] = join(near, far)
         for f in (0, 1):
             hop("k", 2, s, f)
@@ -301,13 +309,14 @@
 
     def t_relay(a, half, q):
         ref, n = shared[a], f"{a}{half}"
-        width = ref.shape[-1] // 2
+        width = ref.shape[-1]
+        cut = (width // 2 + 127) // 128 * 128
         if q == 2:
             got(f"{n}l+", f"{n}l-")
         else:
             s, to, i = ("+", y_next, 0) if q == 1 else ("-", y_prev, 1)
             got(f"{n}{s}")
-            cols = pl.ds(width * i, width)
+            cols = pl.ds(cut * i, cut if i == 0 else width - cut)
             send(f"{n}l{s}", ref.at[q, half, xh, co, :, cols], ref.at[2, half, xh, co, :, cols], to)
         mine = ref.at[q, half, xh, co]
         send(f"{n}x{q}", mine, mine, other_hi, ref.at[q, half, 1 - xh, co])
@@ -376,7 +385,7 @@
         whole = ref[pl.ds(0, T), cols].astype(F32) + plus[3, :, cols].astype(F32) + minus[3, :, cols].astype(F32)
         mine[a, f] = jnp.where(xl == 0, whole[:24], whole[24:])
         theirs = jnp.where(xl == 0, whole[24:], whole[:24])
-        ys[i, f] = jnp.concatenate([theirs, pad[:, :HD]], axis=0).astype(BF)
+        ys[i, f] = jnp.concatenate([theirs, pad], axis=0).astype(BF)
         send(f"{a}e{f}", ys.at[i, f], yr.at[i, f], other_lo)
 
     def t_result(a, out, base, sign):
@@ -514,6 +523,7 @@
     D, F = gate_weight.shape
     Q = D // 4
     T = 48
+    tokens = kept_half.shape[0]
     hbm = pl.BlockSpec(memory_space=pl.ANY)
     vmem = pl.BlockSpec(memory_space=pltpu.VMEM)
 
@@ -523,7 +533,7 @@
     scratch = [
         *[buf(24, D)] * 4,
         buf(D, 2 * F), buf(F, D), buf(2 * F, D), buf(D, F),
-        buf(2, 32, D), buf(2, 32, D), buf(2, 2, 32, D),
+        *[buf(2, 2 * tokens, D // 2)] * 2, buf(2, 2, 2 * tokens, D // 2),
         buf(384, D), buf(384, D),
         buf(3, D, 128), buf(3, D, 128),
         buf(4, 3, Q, 128), buf(4, 3, Q, 128),
@@ -539,7 +549,6 @@
         pltpu.SemaphoreType.DMA((MESSAGES,)),
         pltpu.SemaphoreType.DMA((7,)),
     ]
-    tokens = kept_half.shape[0]
     results = pl.pallas_call(
         kernel,
         out_shape=(buf(tokens, D), buf(tokens, D), buf(Q, 2 * F), buf(Q, F)),

time: 89 us -> 85.5 us (0.961)
  Pallas kernels: 88.1 us -> 84.5 us
    pallas_call x1, Pallas kernels: 86.6 us -> 83 us  [body(): pl.pallas_call(kernel, out_shape=(buf(tokens, D), buf(tokens, D), buf(Q,...]
where the time goes in v5:
time: 85.5 us; the launch traced here: 85.4 us
  Pallas kernels  84.5 us (99%)
    pallas_call x1, Pallas kernels, body(): pl.pallas_call(kernel, out_shape=(buf(tokens, D), buf(tokens, D), buf(Q,...  83 us

profile of v5, /device:TPU:1, one launch (start us, length us, event | category | flops | bytes accessed | tf_op | source)
XLA Modules:
  0.0 85.4 jit_solution(12850940901170100539)
XLA Ops:
  0.6 83.0 %shard_map.110 = (bf16[24,1792]{1,0:T(8,128)(2,1)S(1)}, bf16[24,1792]{1,0:T(8,128)(2,1)S(1)}, bf16[448,1792]{1,0:T(8,128)(2,1)S(1)}, bf16[448,896]{1,0:T(8,128)(2,1)S(1)}) custom-call(bf16[24,1792]{1,0:T(8,128)(2,1)} %kept_hbm.1, bf16[24,1792]{1,0:T(8,128)(2,1)} %mixed_hbm.1, bf16[24,1792]{1,0:T(8,128)(2,1)} %gkept_hbm.1, bf16[24,1792]{1,0:T(8,128)(2,1)} %gmixed_hbm.1, ...), custom_call_target="tpu_custom_call" | custom-call | tf_op jit(solution)/shard_map/pallas_call | solution.py:552
  83.7 1.5 %shard_map.111 = (bf16[24,1792]{1,0:T(8,128)(2,1)}, bf16[24,1792]{1,0:T(8,128)(2,1)}, bf16[1,448,896]{2,1,0:T(8,128)(2,1)}, bf16[1,448,896]{2,1,0:T(8,128)(2,1)}, bf16[448,896]{1,0:T(8,128)(2,1)}) custom-call(bf16[24,1792]{1,0:T(8,128)(2,1)S(1)} %get-tuple-element.14.restored, bf16[24,1792]{1,0:T(8,128)(2,1)S(1)} %get-tuple-element.15.grad_input, ...), custom_call_target="tpu_custom_call" | custom-call | tf_op jit(solution)/shard_map/pallas_call | solution.py:562
